TPU v7x, 32 devices: a whole 2x2x4 slice. The times are simulated.
32 devices in a mesh: ctx: 16 (over z, x, core), head: 2 (over y).
Axes of the slice: x: 2, y: 2, z: 4, core: 2. Of those that a mesh axis runs over, the one named last changes fastest.
Arguments:
- tokens: bfloat16 [12288, 1024], P('ctx')
- qkv_weight: bfloat16 [1024, 3, 1024], P('ctx', None, 'head'), may hold values from -0.1875 to 0.1875
- grad_attn: bfloat16 [12288, 1024], P('ctx', 'head'), may hold values from -6 to 6
- positions: int32 [12288], P('ctx'), may hold values from 0 to 786431, as said below
- slopes: float32 [16], P('head'), may hold values from 0.03 to 0.6
Outputs:
- d_tokens: bfloat16 [12288, 1024], P('ctx')
- d_weight: float32 [1024, 3, 1024], P('ctx', None, 'head')
Inputs may be any that keep to these rules, and one draw needn't show every extreme that they name: positions rise strictly along the sequence, start at 0 and end at 786431; neighbours differ by 1 to 127.
All inputs are finite; a program needn't handle non-finite values.
Results may differ from a plain program's by a relative error of at most 0.006.
The roundings to bfloat16 on the way count: a program that leaves them out, or rounds other values in their place, can miss the bound.
Values may be sent and summed in bfloat16 or wider, within the bound.
A program may use at most 128 MiB of HBM per device.

v0:
```python
import jax
import jax.numpy as jnp
from jax import lax
from jax.sharding import PartitionSpec as P


def from_partner(value, axis, apart):
    mask = 2**apart
    pairs = [(source, source ^ mask) for source in range(lax.axis_size(axis))]
    return lax.ppermute(value, axis, pairs)


def one_head_grads(items, logd, scale):
    q_head, k_head, v_head, g_head, slope = items
    score = (
        jnp.einsum("qe,ke->qk", q_head, k_head, preferred_element_type=jnp.float32) * scale
        - slope * logd
    )
    top = jnp.max(score, axis=-1, keepdims=True)
    expd = jnp.exp(score - top)
    prob = expd / jnp.sum(expd, axis=-1, keepdims=True)
    prob_round = prob.astype(jnp.bfloat16)
    outv = jnp.dot(prob_round, v_head, preferred_element_type=jnp.float32)
    delta = jnp.sum(g_head.astype(jnp.float32) * outv, axis=-1, keepdims=True)
    dprob = jnp.einsum("qe,ke->qk", g_head, v_head, preferred_element_type=jnp.float32)
    dscore = (prob * (dprob - delta) * scale).astype(jnp.bfloat16)
    dq = jnp.dot(dscore, k_head, preferred_element_type=jnp.float32).astype(jnp.bfloat16)
    dk = jnp.einsum("qk,qe->ke", dscore, q_head, preferred_element_type=jnp.float32)
    dv = jnp.einsum("qk,qe->ke", prob_round, g_head, preferred_element_type=jnp.float32)
    return (dq, dk, dv)


def on_device(tokens, qkv_weight, grad_attn, positions, slopes):
    rows = tokens.shape[0]
    heads_local = slopes.shape[0]
    local_width = qkv_weight.shape[2]
    head_size = local_width // heads_local
    scale = head_size ** (-0.5)
    full_weight = lax.all_gather(qkv_weight, "ctx", axis=0, tiled=True)
    qkv = jnp.einsum("sd,dcf->scf", tokens, full_weight, preferred_element_type=jnp.float32).astype(
        jnp.bfloat16
    )

    def split_heads(array):
        return array.reshape(rows, heads_local, head_size).transpose(1, 0, 2)

    def merge_heads(array):
        return array.transpose(1, 0, 2).reshape(rows, local_width)

    top_bit = lax.axis_size("ctx").bit_length() - 2
    far_keys, far_values, far_pos = from_partner((qkv[:, 1], qkv[:, 2], positions), "ctx", top_bit)
    keys_all = jnp.concatenate([split_heads(qkv[:, 1]), split_heads(far_keys)], 1)
    values_all = jnp.concatenate([split_heads(qkv[:, 2]), split_heads(far_values)], 1)
    pos_all = jnp.concatenate([positions, far_pos], 0)
    logd = jnp.log1p(jnp.abs(positions[:, None] - pos_all[None, :]).astype(jnp.float32))

    def per_head(items):
        return one_head_grads(items, logd, scale)

    dq, dk_all, dv_all = lax.map(
        per_head, (split_heads(qkv[:, 0]), keys_all, values_all, split_heads(grad_attn), slopes)
    )
    back_keys, back_values = from_partner((dk_all[:, rows:], dv_all[:, rows:]), "ctx", top_bit)
    dk = (dk_all[:, :rows] + back_keys).astype(jnp.bfloat16)
    dv = (dv_all[:, :rows] + back_values).astype(jnp.bfloat16)
    dqkv = jnp.stack([merge_heads(dq), merge_heads(dk), merge_heads(dv)], 1)
    partial_rows = jnp.einsum("scf,dcf->sd", dqkv, full_weight, preferred_element_type=jnp.float32)
    d_tokens = lax.psum(partial_rows, "head").astype(jnp.bfloat16)
    term = jnp.einsum("sd,scf->dcf", tokens, dqkv, preferred_element_type=jnp.float32)
    d_weight = lax.psum_scatter(term, "ctx", scatter_dimension=0, tiled=True)
    return (d_tokens, d_weight)


def solution(mesh):
    placed = (P("ctx", None), P("ctx", None, "head"), P("ctx", "head"), P("ctx"), P("head"))
    return jax.shard_map(
        on_device,
        mesh=mesh,
        in_specs=placed,
        out_specs=(P("ctx", None), P("ctx", None, "head")),
        check_vma=False,
    )
```

profile of v0, /device:TPU:0, one launch (start us, length us, event | category | flops | bytes accessed | tf_op | source)
XLA Modules:
  0.0 619.7 jit_solution(10123760618341573433)
XLA Ops:
  8.0 50.2 %all-gather.2.cloned.1.call-done = bf16[1024,3,512]{2,0,1:T(8,128)(2,1)} async-done(((bf16[64,3,512]{2,0,1:T(8,128)(2,1)}), bf16[1024,3,512]{2,0,1:T(8,128)(2,1)}) %all-gather.2.cloned.1.call-update) | async-done | bytes 3145744 | tf_op jit(solution)/shard_map/all_gather | solution.py:39
  58.1 4.5 convolution_convert_fusion.1
  70.9 65.1 %collective-permute-done.1 = s32[768]{0:T(1024)S(1)} collective-permute-done((s32[768]{0:T(1024)S(1)}, s32[768]{0:T(1024)S(1)}, u32[]{:S(2)}, u32[]{:S(2)}) %collective-permute-start.1) | collective-permute-done | bytes 3104 | tf_op jit(solution)/shard_map/ppermute | solution.py:10
  136.1 2.6 copy.33
  142.7 2.5 copy.34
  147.6 5.2 pad_maximum_fusion
  152.8 131.1 %while.15 = (s32[]{:T(128)}, bf16[8,768,64]{1,2,0:T(8,128)(2,1)S(1)}, f32[8,1536,64]{1,2,0:T(8,128)}, f32[8,1536,64]{1,2,0:T(8,128)}, bf16[8,768,64]{2,1,0:T(8,1...) while((s32[]{:T(128)}, ...), condition=%wide.region_4.5_spmd.clone, body=%wide.region_0.4_spmd.clone.sunk | while | flops 926217984 | bytes 43292288 | solution.py:60
  153.4 4.6 fusion.77
  169.7 4.6 fusion.77
  186.1 4.6 fusion.77
  202.5 4.6 fusion.77
  218.8 4.6 fusion.77
  235.2 4.6 fusion.77
  251.6 4.6 fusion.77
  268.0 4.6 fusion.77
  286.4 2.7 slice.29
  289.1 2.9 collective-permute-start.4
  295.5 94.7 %collective-permute-done.3 = f32[8,768,64]{1,2,0:T(8,128)} collective-permute-done((f32[8,768,64]{1,2,0:T(8,128)S(1)}, f32[8,768,64]{1,2,0:T(8,128)}, u32[]{:S(2)}, u32[]{:S(2)}) %collective-permute-start.3) | collective-permute-done | bytes 1572896 | tf_op jit(solution)/shard_map/ppermute | solution.py:10
  393.4 30.4 %collective-permute-done.4 = f32[8,768,64]{1,2,0:T(8,128)} collective-permute-done((f32[8,768,64]{1,2,0:T(8,128)}, f32[8,768,64]{1,2,0:T(8,128)}, u32[]{:S(2)}, u32[]{:S(2)}) %collective-permute-start.4) | collective-permute-done | bytes 1572896 | tf_op jit(solution)/shard_map/ppermute | solution.py:10
  427.0 6.0 convolution_bitcast_fusion.2
  433.0 9.4 %copy.39 = f32[1024,3,512]{2,1,0:T(4,128)} copy(f32[1024,3,512]{0,2,1:T(8,128)} %convolution_bitcast_fusion.2) | data formatting | bytes 12582912 | tf_op jit(solution)/shard_map/sd,scf->dcf/dot_general | solution.py:69
  443.5 6.5 %convolution_bitcast_fusion.3 = f32[768,1024]{1,0:T(8,128)} fusion(bf16[1024,3,512]{2,0,1:T(8,128)(2,1)} %all-gather.2.cloned.1.call-done, bf16[768,1,512]{2,0,1:T(8,128)(2,1)} %copy.37, bf16[768,1,512]{2,0,1:T(8,128)(2,1)S(1)} %copy-done.4, bf16[768,1,512]{2,0,1:T(8,128)(2,1)S(1)} %copy-done.3), kind=kOutput, calls=%fused_computation.46 | convolution fusion | flops 2418278400 | bytes 8650752 | tf_op jit(solution)/shard_map/scf,dcf->sd/dot_general | solution.py:67
  450.0 77.8 %all-reduce.5 = bf16[768,1024]{1,0:T(8,128)(2,1)} all-reduce(f32[768,1024]{1,0:T(8,128)} %convolution_bitcast_fusion.3), channel_id=1, replica_groups=mesh['ctx'=16,'head'=2] {'head'}, use_global_device_ids=true, to_apply=%region_5.6 | all-reduce | flops 786432 | bytes 4718592 | tf_op jit(solution)/shard_map/psum | solution.py:68
  527.8 83.1 %all-reduce.4.cloned.1.call-done = f32[1024,3,512]{2,1,0:T(4,128)} async-done(((f32[1024,3,512]{2,1,0:T(4,128)}), f32[1024,3,512]{2,1,0:T(4,128)}) %all-reduce.4.cloned.1.call-update) | async-done | bytes 6291472
  (108 shorter events, 124.3 us)
Async XLA Ops:
  7.2 51.0 %copy-start = (bf16[768,1024]{1,0:T(8,128)(2,1)S(1)}, bf16[768,1024]{1,0:T(8,128)(2,1)}, u32[]{:S(2)}) copy-start(bf16[768,1024]{1,0:T(8,128)(2,1)} %param.7) | copy-start | bytes 4718596
  7.2 51.0 %all-gather.2.cloned.1.call-start = ((), (), s32[]{:S(2)}) async-start(), calls=%async_computation | async-start | bytes 3342336 | tf_op jit(solution)/shard_map/all_gather | solution.py:39
  7.9 603.0 %all-reduce.4.cloned.1.call-start = ((), (), s32[]{:S(2)}) async-start(), calls=%async_computation.1 | async-start | bytes 16777216
  62.7 4.7 copy-start.5
  64.5 78.2 %collective-permute-start.2 = (bf16[768,512]{0,1:T(8,128)(2,1)}, bf16[768,512]{0,1:T(8,128)(2,1)}, u32[]{:S(2)}, u32[]{:S(2)}) collective-permute-start(bf16[768,512]{0,1:T(8,128)(2,1)} %get-tuple-element.117), channel_id=1, source_target_pairs={{0,16},{2,18},{4,20},{6,22},{8,24},{10,26},{12,28},{14,30},{16,0},... | collective-permute-start | bytes 2359304 | tf_op jit(solution)/shard_map/ppermute | solution.py:10
  66.6 78.6 %collective-permute-start = (bf16[768,512]{0,1:T(8,128)(2,1)}, bf16[768,512]{0,1:T(8,128)(2,1)}, u32[]{:S(2)}, u32[]{:S(2)}) collective-permute-start(bf16[768,512]{0,1:T(8,128)(2,1)} %get-tuple-element.116), channel_id=1, source_target_pairs={{0,16},{2,18},{4,20},{6,22},{8,24},{10,26},{12,28},{14,30},{16,0},... | collective-permute-start | bytes 2359304 | tf_op jit(solution)/shard_map/ppermute | solution.py:10
  67.4 68.7 %collective-permute-start.1 = (s32[768]{0:T(1024)S(1)}, s32[768]{0:T(1024)S(1)}, u32[]{:S(2)}, u32[]{:S(2)}) collective-permute-start(s32[768]{0:T(1024)S(1)} %copy-done.5), channel_id=1, source_target_pairs={{0,16},{2,18},{4,20},{6,22},{8,24},{10,26},{12,28},{14,30},{16,0},... | collective-permute-start | bytes 9224 | tf_op jit(solution)/shard_map/ppermute | solution.py:10
  147.6 5.2 copy-start.1
  147.6 5.2 copy-start.6
  283.9 0.9 copy-start.2
  284.8 7.2 %copy-start.7 = (u32[32]{0:T(128)S(1)}, u32[32]{0:T(128)}, u32[]{:S(2)}) copy-start(u32[32]{0:T(128)} %constant.30) | copy-start | bytes 388
  286.3 103.9 %collective-permute-start.3 = (f32[8,768,64]{1,2,0:T(8,128)S(1)}, f32[8,768,64]{1,2,0:T(8,128)}, u32[]{:S(2)}, u32[]{:S(2)}) collective-permute-start(f32[8,768,64]{1,2,0:T(8,128)S(1)} %slice.27), channel_id=1, source_target_pairs={{0,16},{2,18},{4,20},{6,22},{8,24},{10,26},{12,28},{14,30},{16,0},... | collective-permute-start | bytes 4718600 | tf_op jit(solution)/shard_map/ppermute | solution.py:10
  289.1 134.7 %collective-permute-start.4 = (f32[8,768,64]{1,2,0:T(8,128)}, f32[8,768,64]{1,2,0:T(8,128)}, u32[]{:S(2)}, u32[]{:S(2)}) collective-permute-start(f32[8,768,64]{1,2,0:T(8,128)} %slice.29), channel_id=1, source_target_pairs={{0,16},{2,18},{4,20},{6,22},{8,24},{10,26},{12,28},{14,30},{16,0},... | collective-permute-start | bytes 4718600 | tf_op jit(solution)/shard_map/ppermute | solution.py:10
  393.4 33.6 %copy-start.3 = (bf16[768,1,512]{2,0,1:T(8,128)(2,1)S(1)}, bf16[768,1,512]{2,0,1:T(8,128)(2,1)}, u32[]{:S(2)}) copy-start(bf16[768,1,512]{2,0,1:T(8,128)(2,1)} %copy.35) | copy-start | bytes 2359300
  442.4 1.1 copy-start.4
Sparse Core Ops, SparseCore 0:
  10.2 47.8 all-gather.1
  442.5 168.2 all-reduce.3
where the time goes:
time: 622 us; the launch traced here: 620 us
  waiting for transfers between devices  324 us (52%)
  matrix products  129 us (21%)
  blocking collectives  77.8 us (13%)
  local copies, waits for them, and re-layouts  42 us (7%)
  other arithmetic  23.2 us (4%)
  between operations  14.8 us (2%)
  starting transfers between devices  8.1 us (1%)
    ppermute x5, waiting for transfers between devices, from_partner(): return lax.ppermute(value, axis, pairs)  190 us
    unnamed x3, waiting for transfers between devices  83.8 us
    psum x1, blocking collectives, on_device(): d_tokens = lax.psum(partial_rows, 'head').astype(jnp.bfloat16)  77.8 us
    all_gather x1, waiting for transfers between devices, on_device(): full_weight = lax.all_gather(qkv_weight, 'ctx', axis=0, tiled=True)  50.2 us
    dot_general x8, matrix products, one_head_grads(): jnp.einsum('qe,ke->qk', q_head, k_head, preferred_element_type=jnp.float32)  36.9 us
    dot_general x8, matrix products, one_head_grads(): jnp.einsum('qk,qe->ke', dscore, q_head, preferred_element_type=jnp.float32)  18.3 us
    dot_general x8, matrix products, one_head_grads(): jnp.einsum('qe,ke->qk', g_head, v_head, preferred_element_type=jnp.float32)  16.9 us
    dot_general x8, matrix products, one_head_grads(): outv = jnp.dot(prob_round, v_head, preferred_element_type=jnp.float32)  15 us
  transfers between devices with their start and end apart: 7, of which 5 were waited for; matrix products, arithmetic and copies ran while one was open for 4% of the time, Pallas kernels for 0%

commit v1 on v0

v1 whole, which is shorter than its diff:
```python
import functools
import math

import jax
import jax.numpy as jnp
from jax import lax
from jax.experimental import pallas as pl
from jax.experimental.pallas import tpu as pltpu
from jax.sharding import PartitionSpec as P

F32 = jnp.float32
BF16 = jnp.bfloat16
LOG2E = math.log2(math.e)
PAIR = 128
TILE = 256


def flip(value, axis, mask):
    pairs = [(source, source ^ mask) for source in range(lax.axis_size(axis))]
    return lax.ppermute(value, axis, pairs)


def ordered(mine, other, bit):
    first = jnp.concatenate([mine, other], 0)
    second = jnp.concatenate([other, mine], 0)
    return jnp.where(bit == 0, first, second)


def attention_kernel(slope_ref, q_ref, k_ref, kt_ref, v_ref, g_ref, logd_ref, own_ref, far_ref, dk_acc, dv_acc):
    step = pl.program_id(0)
    steps = pl.num_programs(0)
    half = steps // 2
    size = PAIR // 2
    rows = own_ref.shape[1]
    scale = size ** (-0.5)

    @pl.when(step == 0)
    def _():
        dk_acc[...] = jnp.zeros_like(dk_acc)
        dv_acc[...] = jnp.zeros_like(dv_acc)

    lane = lax.broadcasted_iota(jnp.int32, (TILE, PAIR), 1)
    key = k_ref[...]
    key_t = kt_ref[...]
    value = v_ref[...]
    query = q_ref[...].astype(F32)
    grad = g_ref[...].astype(F32)
    contract_last = (((1,), (1,)), ((), ()))
    grads_q = []
    for head in range(2):
        here = (lane >= head * size) & (lane < (head + 1) * size)
        q_head = jnp.where(here, query, 0.0).astype(BF16)
        g_head = jnp.where(here, grad, 0.0)
        g_scaled = (g_head * scale).astype(BF16)
        g_head = g_head.astype(BF16)
        score = lax.dot_general(key, q_head, contract_last, preferred_element_type=F32)
        score = score * (scale * LOG2E) - logd_ref[...] * slope_ref[head]
        top = jnp.max(score, axis=0, keepdims=True)
        expd = jnp.exp2(score - top)
        inverse = 1.0 / jnp.sum(expd, axis=0, keepdims=True)
        prob = expd * inverse
        prob_round = prob.astype(BF16)
        dprob = lax.dot_general(value, g_scaled, contract_last, preferred_element_type=F32)
        delta = jnp.sum(prob_round.astype(F32) * dprob, axis=0, keepdims=True)
        dscore = (prob * (dprob - delta)).astype(BF16)
        dv_acc[...] += jnp.dot(prob_round, g_head, preferred_element_type=F32)
        dk_acc[...] += jnp.dot(dscore, q_head, preferred_element_type=F32)
        grad_q = jnp.dot(key_t, dscore, preferred_element_type=F32)
        grads_q.append(grad_q[head * size : (head + 1) * size])
    grad_q = jnp.concatenate(grads_q, 0).T.astype(BF16)

    @pl.when(step < half)
    def _():
        own_ref[0, pl.ds(pl.multiple_of(step * TILE, TILE), TILE), :] = grad_q

    @pl.when(step >= half)
    def _():
        far_ref[0, pl.ds(pl.multiple_of((step - half) * TILE, TILE), TILE), :] = grad_q

    @pl.when(step == steps - 1)
    def _():
        own_ref[1] = dk_acc[:rows].astype(BF16)
        own_ref[2] = dv_acc[:rows].astype(BF16)
        far_ref[1] = dk_acc[rows:].astype(BF16)
        far_ref[2] = dv_acc[rows:].astype(BF16)


def attention(pair, slopes, qkv, keys_t, grad, logd):
    both, width = qkv.shape
    rows = both // 2
    groups = width // (3 * PAIR)
    out = jax.ShapeDtypeStruct((3, rows, PAIR), BF16)
    whole = pl.BlockSpec((3, rows, PAIR), lambda i: (0, 0, 0))
    return pl.pallas_call(
        attention_kernel,
        grid=(both // TILE,),
        out_shape=(out, out),
        in_specs=[
            pl.BlockSpec(memory_space=pltpu.SMEM),
            pl.BlockSpec((TILE, PAIR), lambda i: (i, pair)),
            pl.BlockSpec((both, PAIR), lambda i: (0, groups + pair)),
            pl.BlockSpec((PAIR, both), lambda i: (pair, 0)),
            pl.BlockSpec((both, PAIR), lambda i: (0, 2 * groups + pair)),
            pl.BlockSpec((TILE, PAIR), lambda i: (i, pair)),
            pl.BlockSpec((both, TILE), lambda i: (0, i)),
        ],
        out_specs=(whole, whole),
        scratch_shapes=[pltpu.VMEM((both, PAIR), F32), pltpu.VMEM((both, PAIR), F32)],
        compiler_params=pltpu.CompilerParams(vmem_limit_bytes=48 * 2**20),
        cost_estimate=pl.CostEstimate(
            flops=12 * both * both * PAIR * 2, bytes_accessed=4 * both * both, transcendentals=2 * both * both
        ),
    )(slopes[2 * pair : 2 * pair + 2], qkv, qkv, keys_t, qkv, grad, logd)


def on_device(tokens, qkv_weight, grad_attn, positions, slopes):
    rows, model = tokens.shape
    blocks = lax.axis_size("ctx")
    far_mask = blocks // 2
    bits = far_mask.bit_length() - 1
    me = lax.axis_index("ctx")
    side = me // far_mask
    head_side = lax.axis_index("head")
    shard, _, local_width = qkv_weight.shape
    width = local_width // 2
    heads = slopes.shape[0] // 2
    pairs = width // PAIR
    half_rows = rows // 2

    def bit_of(position):
        return (me // 2**position) % 2

    with jax.named_scope("exchange_inputs"):
        weight_parts = [
            lax.dynamic_slice_in_dim(qkv_weight, which * width, width, 2).reshape(shard, 3 * width)
            for which in (side, 1 - side)
        ]
        far_positions = flip(positions, "ctx", far_mask)
        other_weight = flip(weight_parts[1], "ctx", far_mask)
        token_half = lax.dynamic_slice_in_dim(tokens, head_side * half_rows, half_rows, 0)
        quarter = half_rows // 2
        near, cross = [], []
        for part in range(2):
            arrived = flip(token_half[part * quarter : (part + 1) * quarter], "ctx", far_mask)
            near.append(arrived)
            cross.append(flip(arrived, "head", 1))
        far_tokens = ordered(jnp.concatenate(near, 0), jnp.concatenate(cross, 0), head_side)
        grad_mine = lax.dynamic_slice_in_dim(grad_attn, side * width, width, 1)
        far_grad = flip(lax.dynamic_slice_in_dim(grad_attn, (1 - side) * width, width, 1), "ctx", far_mask)
        grad = jnp.concatenate([grad_mine, far_grad], 0)
        slopes_mine = lax.dynamic_slice_in_dim(slopes, side * heads, heads, 0)

    def gather_weight(mine, other):
        stacked = ordered(mine[None], other[None], side)[:, None]
        for position in reversed(range(bits)):
            arrived = flip(stacked, "ctx", 2**position)
            pieces = (stacked[:, :, None], arrived[:, :, None])
            along = [jnp.concatenate(c, 2) for c in (pieces, pieces[::-1])]
            stacked = jnp.where(bit_of(position) == 0, along[0], along[1])
            stacked = stacked.reshape(2, -1, shard, 3 * width)
        return stacked.reshape(model, 3 * width)

    with jax.named_scope("gather_weight"):
        weight = gather_weight(weight_parts[0], other_weight)

    with jax.named_scope("log_distance"):
        pos = jnp.concatenate([positions, far_positions], 0)
        logd = jnp.log(jnp.abs(pos[:, None] - pos[None, :]).astype(F32) + 1.0) * LOG2E

    with jax.named_scope("project"):
        qkv_own = jnp.dot(tokens, weight, preferred_element_type=F32).astype(BF16)
        qkv_far = jnp.dot(far_tokens, weight, preferred_element_type=F32).astype(BF16)
        qkv = jnp.concatenate([qkv_own, qkv_far], 0)
        keys_t = qkv[:, width : 2 * width].T
        both_tokens = jnp.concatenate([tokens, far_tokens], 0)

    with jax.named_scope("gather_other_weight"):
        late = lax.optimization_barrier((weight_parts[0], weight_parts[1], qkv_own))
        back_weight = flip(late[0], "ctx", far_mask)
        weight_other = gather_weight(late[1], back_weight)

    def reduce_weight(term):
        total = term.reshape(2, far_mask, shard, term.shape[1])
        for position in range(bits):
            bit = bit_of(position)
            folded = total.reshape(2, total.shape[1] // 2, 2, shard, term.shape[1])
            send = lax.dynamic_index_in_dim(folded, 1 - bit, 2, keepdims=False)
            keep = lax.dynamic_index_in_dim(folded, bit, 2, keepdims=False)
            total = keep + flip(send, "ctx", 2**position)
        total = total.reshape(2, shard, term.shape[1])
        keep = lax.dynamic_index_in_dim(total, side, 0, keepdims=False)
        arrived = flip(lax.dynamic_index_in_dim(total, 1 - side, 0, keepdims=False), "ctx", far_mask)
        return keep, arrived

    own, other, terms = [], [], []
    for pair in range(pairs):
        with jax.named_scope("attention"):
            mine, theirs = attention(pair, slopes_mine, qkv, keys_t, grad, logd)
        with jax.named_scope("return_grads"):
            own.append(mine)
            other.append(flip(theirs, "ctx", far_mask))
        with jax.named_scope("weight_grad"):
            stacked = jnp.concatenate([mine, theirs], 1)
            term = jnp.einsum("sd,csf->dcf", both_tokens, stacked, preferred_element_type=F32)
            terms.append(reduce_weight(term.reshape(model, 3 * PAIR)))

    with jax.named_scope("token_grad"):
        dqkv = jnp.concatenate(own + other, 0)
        joined = []
        for array in (weight, weight_other):
            array = array.reshape(model, 3, pairs, PAIR)
            joined.append(array.transpose(2, 1, 0, 3).reshape(3 * pairs, model, PAIR))
        joined = jnp.concatenate(joined, 0)

        def partial_rows(part):
            rows_part = lax.dynamic_slice_in_dim(dqkv, part * half_rows, half_rows, 1)
            return jnp.einsum("csf,cdf->sd", rows_part, joined, preferred_element_type=F32)

        sent = partial_rows(1 - head_side)
        kept = partial_rows(head_side)
        mine, cross = [], []
        for part in range(2):
            cut = slice(part * quarter, (part + 1) * quarter)
            total = (kept[cut] + flip(sent[cut], "head", 1)).astype(BF16)
            mine.append(total)
            cross.append(flip(total, "head", 1))
        d_tokens = ordered(jnp.concatenate(mine, 0), jnp.concatenate(cross, 0), head_side)

    with jax.named_scope("weight_grad_out"):
        keep = jnp.stack([t[0].reshape(shard, 3, PAIR) for t in terms], 2).reshape(shard, 3, width)
        arrived = jnp.stack([t[1].reshape(shard, 3, PAIR) for t in terms], 2).reshape(shard, 3, width)
        d_weight = jnp.where(
            side == 0, jnp.concatenate([keep, arrived], 2), jnp.concatenate([arrived, keep], 2)
        )
    return (d_tokens, d_weight)


def solution(mesh):
    placed = (P("ctx", None), P("ctx", None, "head"), P("ctx", "head"), P("ctx"), P("head"))
    return jax.shard_map(
        on_device,
        mesh=mesh,
        in_specs=placed,
        out_specs=(P("ctx", None), P("ctx", None, "head")),
        check_vma=False,
    )
```

time: 622 us -> 300 us (0.48)
  waiting for transfers between devices: 324 us -> 144 us
  matrix products: 129 us -> 15.1 us
  blocking collectives: 77.8 us -> 0 us
  Pallas kernels: 0 us -> 54.7 us
  starting transfers between devices: 8.1 us -> 30.5 us
  between operations: 14.8 us -> 1.33 us
    dot_general x51 -> x6, matrix products: 129 us -> 15.1 us  [the longest x2 6.93 us: on_device(): jnp.einsum('sd,csf->dcf', both_tokens, stacked, preferred_element_type=F32)]
    unnamed x3 -> x0, waiting for transfers between devices: 83.8 us -> none
    psum x1 -> x0, blocking collectives: 77.8 us -> none  [on_device(): d_tokens = lax.psum(partial_rows, 'head').astype(jnp.bfloat16)]
    pallas_call x0 -> x2, Pallas kernels: none -> 54.7 us  [attention(): pl.pallas_call(attention_kernel, grid=(both // TILE,), out_shape=(out, ou...]
    all_gather x1 -> x0, waiting for transfers between devices: 50.2 us -> none  [on_device(): full_weight = lax.all_gather(qkv_weight, 'ctx', axis=0, tiled=True)]
    ppermute x5 -> x28, waiting for transfers between devices: 190 us -> 144 us  [flip(): return lax.ppermute(value, axis, pairs)]
    ppermute x5 -> x28, starting transfers between devices: 8.03 us -> 30.5 us  [flip(): return lax.ppermute(value, axis, pairs)]
    another operation x6 -> x2, local copies, waits for them, and re-layouts: 11.3 us -> 0.31 us  [the longest x1 0.15 us: on_device(): jnp.stack([t[1].reshape(shard, 3, PAIR) for t in terms], 2)]
  transfers between devices with their start and end apart: 7 -> 28, of which waited for: 5 -> 13; matrix products, arithmetic and copies ran while one was open for 4% -> 18% of each run, Pallas kernels for 0% -> 18%
where the time goes in v1:
time: 300 us; the launch traced here: 299 us
  waiting for transfers between devices  144 us (48%)
  Pallas kernels  54.7 us (18%)
  local copies, waits for them, and re-layouts  36.7 us (12%)
  starting transfers between devices  30.5 us (10%)
  other arithmetic  17 us (6%)
  matrix products  15.1 us (5%)
    ppermute x28, waiting for transfers between devices, flip(): return lax.ppermute(value, axis, pairs)  144 us
    pallas_call x2, Pallas kernels, attention(): pl.pallas_call(attention_kernel, grid=(both // TILE,), out_shape=(out, ou...  54.7 us
    ppermute x28, starting transfers between devices, flip(): return lax.ppermute(value, axis, pairs)  30.5 us
    unnamed x49, local copies, waits for them, and re-layouts  7.27 us
    dot_general x2, matrix products, on_device(): jnp.einsum('sd,csf->dcf', both_tokens, stacked, preferred_element_type=F32)  6.93 us
  transfers between devices with their start and end apart: 28, of which 13 were waited for; matrix products, arithmetic and copies ran while one was open for 18% of the time, Pallas kernels for 18%

profile of v1, /device:TPU:0, one launch (start us, length us, event | category | flops | bytes accessed | tf_op | source)
XLA Modules:
  0.0 299.5 jit_solution(3517343242020493756)
XLA Ops:
  0.6 4.1 %collective-permute-start.9 = (s32[768]{0:T(1024)}, s32[768]{0:T(1024)S(1)}, u32[]{:S(2)}, u32[]{:S(2)}) collective-permute-start(s32[768]{0:T(1024)} %param.8), channel_id=1, source_target_pairs={{0,16},{2,18},{4,20},{6,22},{8,24},{10,26},{12,28},{14,30},{16,0},... | collective-permute-start | bytes 9224 | tf_op jit(solution)/shard_map/exchange_inputs/ppermute | solution.py:20
  7.1 2.8 collective-permute-start.8
  11.0 2.8 collective-permute-start.5
  14.1 25.4 %collective-permute-done = bf16[64,768]{1,0:T(8,128)(2,1)S(1)} collective-permute-done((bf16[64,768]{1,0:T(8,128)(2,1)S(1)}, bf16[64,768]{1,0:T(8,128)(2,1)S(1)}, u32[]{:S(2)}, u32[]{:S(2)}) %collective-permute-start) | collective-permute-done | bytes 98336 | tf_op jit(solution)/shard_map/exchange_inputs/ppermute | solution.py:20
  39.7 28.1 %collective-permute-done.1 = bf16[2,1,64,768]{3,2,0,1:T(8,128)(2,1)S(1)} collective-permute-done((bf16[2,1,64,768]{3,2,0,1:T(8,128)(2,1)S(1)}, bf16[2,1,64,768]{3,2,0,1:T(8,128)(2,1)S(1)}, u32[]{:S(2)}, u32[]{:S(2)}) %collective-permute-start.1) | collective-permute-done | bytes 196640 | tf_op jit(solution)/shard_map/gather_weight/ppermute | solution.py:20
  71.8 7.3 %collective-permute-done.2 = bf16[2,2,64,768]{3,2,1,0:T(8,128)(2,1)S(1)} collective-permute-done((bf16[2,2,64,768]{3,2,1,0:T(8,128)(2,1)S(1)}, bf16[2,2,64,768]{3,2,1,0:T(8,128)(2,1)S(1)}, u32[]{:S(2)}, u32[]{:S(2)}) %collective-permute-start.2) | collective-permute-done | bytes 393248 | tf_op jit(solution)/shard_map/gather_weight/ppermute | solution.py:20
  79.3 5.6 %log_multiply_fusion.logd_ref = f32[1536,1536]{1,0:T(8,128)} fusion(s32[1536]{0:T(1024)S(1)} %constant_dynamic-update-slice_fusion.5), kind=kLoop, calls=%fused_computation | loop fusion | flops 11796480 | bytes 9443328 | tf_op jit(solution)/shard_map/log_distance/mul | solution.py:168
  85.9 3.0 collective-permute-done.7
  97.1 4.4 %select_n.304 = bf16[1024,3,2,128]{3,2,1,0:T(2,128)(2,1)} reshape(bf16[2,4,2,64,768]{4,3,2,1,0:T(8,128)(2,1)} %copy-done.7) | data formatting | bytes 3145728 | tf_op jit(solution)/shard_map/gather_weight/jit(_where)/select_n | solution.py:159
  103.8 2.8 copy.75
  106.7 27.1 %attention.3 = (bf16[3,768,128]{2,1,0:T(8,128)(2,1)S(1)}, bf16[3,768,128]{2,1,0:T(8,128)(2,1)}) custom-call(f32[2]{0:T(128)S(1)} %get-tuple-element.30.slope_ref, bf16[1536,768]{1,0:T(8,128)(2,1)S(1)} %pad_maximum_fusion.1.q_ref.k_ref.v_ref, bf16[1536,768]{1,0:T(8,128)(2,1)S(1)} %pad_maximum_fusion.1.q_ref.k_ref.v_ref, bf16[256,1536]{1,0:T(8,128)(2,1)S(1)} %copy-done, ...), custom_call_target="tpu_custom_call" | custom-call | flops 7247757312 | bytes 9437184 | tf_op jit(solution)/shard_map/attention/pallas_call | solution.py:94
  133.7 27.6 %attention.2 = (bf16[3,768,128]{2,1,0:T(8,128)(2,1)S(1)}, bf16[3,768,128]{2,1,0:T(8,128)(2,1)}) custom-call(f32[2]{0:T(128)S(1)} %get-tuple-element.31.slope_ref, bf16[1536,768]{1,0:T(8,128)(2,1)S(1)} %pad_maximum_fusion.1.q_ref.k_ref.v_ref, bf16[1536,768]{1,0:T(8,128)(2,1)S(1)} %pad_maximum_fusion.1.q_ref.k_ref.v_ref, bf16[256,1536]{1,0:T(8,128)(2,1)S(1)} %copy-done, ...), custom_call_target="tpu_custom_call" | custom-call | flops 7247757312 | bytes 9437184 | tf_op jit(solution)/shard_map/attention/pallas_call | solution.py:94
  161.4 2.9 collective-permute-start.11
  164.3 4.1 %fusion = f32[1024,3,128]{2,0,1:T(8,128)} fusion(bf16[768,1024]{1,0:T(8,128)(2,1)S(1)} %copy-done.12, bf16[768,1024]{1,0:T(8,128)(2,1)S(1)} %copy-done.18, bf16[3,768,128]{2,1,0:T(8,128)(2,1)} %get-tuple-element.11, bf16[3,768,128]{2,1,0:T(8,128)(2,1)S(1)} %get-tuple-element.9), kind=kOutput, calls=%fused_computation.6 | convolution fusion | flops 1216610304 | bytes 5898240 | tf_op jit(solution)/shard_map/weight_grad/sd,csf->dcf/dot_general | solution.py:204
  168.4 2.9 fusion.1
  183.7 9.0 %collective-permute-done.13 = bf16[2,1,64,768]{3,2,1,0:T(8,128)(2,1)S(1)} collective-permute-done((bf16[2,1,64,768]{3,2,1,0:T(8,128)(2,1)S(1)}, bf16[2,1,64,768]{3,2,1,0:T(8,128)(2,1)S(1)}, u32[]{:S(2)}, u32[]{:S(2)}) %collective-permute-start.13) | collective-permute-done | bytes 196640 | tf_op jit(solution)/shard_map/gather_other_weight/ppermute | solution.py:20
  193.5 21.1 %collective-permute-done.10 = bf16[3,768,128]{2,1,0:T(8,128)(2,1)} collective-permute-done((bf16[3,768,128]{2,1,0:T(8,128)(2,1)}, bf16[3,768,128]{2,1,0:T(8,128)(2,1)}, u32[]{:S(2)}, u32[]{:S(2)}) %collective-permute-start.10) | collective-permute-done | bytes 589856 | tf_op jit(solution)/shard_map/return_grads/ppermute | solution.py:20
  219.6 9.7 %collective-permute-done.21 = f32[2,2,64,384]{3,2,1,0:T(8,128)S(1)} collective-permute-done((f32[2,2,64,384]{3,2,1,0:T(8,128)S(1)}, f32[2,2,64,384]{3,2,1,0:T(8,128)S(1)}, u32[]{:S(2)}, u32[]{:S(2)}) %collective-permute-start.21) | collective-permute-done | bytes 393248 | tf_op jit(solution)/shard_map/weight_grad/ppermute | solution.py:20
  230.2 6.0 %collective-permute-done.24 = f32[2,2,64,384]{3,2,1,0:T(8,128)S(1)} collective-permute-done((f32[2,2,64,384]{3,2,1,0:T(8,128)S(1)}, f32[2,2,64,384]{3,2,1,0:T(8,128)S(1)}, u32[]{:S(2)}, u32[]{:S(2)}) %collective-permute-start.24) | collective-permute-done | bytes 393248 | tf_op jit(solution)/shard_map/weight_grad/ppermute | solution.py:20
  252.2 2.7 fusion.4
  254.9 9.7 %collective-permute-done.16 = f32[192,1024]{1,0:T(8,128)} collective-permute-done((f32[192,1024]{1,0:T(8,128)}, f32[192,1024]{1,0:T(8,128)}, u32[]{:S(2)}, u32[]{:S(2)}) %collective-permute-start.16) | collective-permute-done | bytes 786464 | tf_op jit(solution)/shard_map/token_grad/ppermute | solution.py:20
  264.6 14.4 %collective-permute-done.17 = f32[192,1024]{1,0:T(8,128)} collective-permute-done((f32[192,1024]{1,0:T(8,128)}, f32[192,1024]{1,0:T(8,128)}, u32[]{:S(2)}, u32[]{:S(2)}) %collective-permute-start.17) | collective-permute-done | bytes 786464 | tf_op jit(solution)/shard_map/token_grad/ppermute | solution.py:20
  289.6 3.2 %collective-permute-done.18 = bf16[192,1024]{1,0:T(8,128)(2,1)S(1)} collective-permute-done((bf16[192,1024]{1,0:T(8,128)(2,1)S(1)}, bf16[192,1024]{1,0:T(8,128)(2,1)S(1)}, u32[]{:S(2)}, u32[]{:S(2)}) %collective-permute-start.18) | collective-permute-done | bytes 393248 | tf_op jit(solution)/shard_map/token_grad/ppermute | solution.py:20
  292.7 5.0 %collective-permute-done.19 = bf16[192,1024]{1,0:T(8,128)(2,1)S(1)} collective-permute-done((bf16[192,1024]{1,0:T(8,128)(2,1)S(1)}, bf16[192,1024]{1,0:T(8,128)(2,1)S(1)}, u32[]{:S(2)}, u32[]{:S(2)}) %collective-permute-start.19) | collective-permute-done | bytes 393248 | tf_op jit(solution)/shard_map/token_grad/ppermute | solution.py:20
  (160 shorter events, 66.5 us)
Async XLA Ops:
  0.6 68.9 %collective-permute-start.9 = (s32[768]{0:T(1024)}, s32[768]{0:T(1024)S(1)}, u32[]{:S(2)}, u32[]{:S(2)}) collective-permute-start(s32[768]{0:T(1024)} %param.8), channel_id=1, source_target_pairs={{0,16},{2,18},{4,20},{6,22},{8,24},{10,26},{12,28},{14,30},{16,0},... | collective-permute-start | bytes 9224 | tf_op jit(solution)/shard_map/exchange_inputs/ppermute | solution.py:20
  5.7 33.8 %collective-permute-start = (bf16[64,768]{1,0:T(8,128)(2,1)S(1)}, bf16[64,768]{1,0:T(8,128)(2,1)S(1)}, u32[]{:S(2)}, u32[]{:S(2)}) collective-permute-start(bf16[64,768]{1,0:T(8,128)(2,1)S(1)} %bitcast.101), channel_id=1, source_target_pairs={{0,16},{2,18},{4,20},{6,22},{8,24},{10,26},{12,28},{14,30},{16,0},... | collective-permute-start | bytes 294920 | tf_op jit(solution)/shard_map/exchange_inputs/ppermute | solution.py:20
  7.1 77.8 %collective-permute-start.8 = (bf16[768,256]{1,0:T(8,128)(2,1)S(1)}, bf16[768,256]{1,0:T(8,128)(2,1)}, u32[]{:S(2)}, u32[]{:S(2)}) collective-permute-start(bf16[768,256]{1,0:T(8,128)(2,1)S(1)} %get-tuple-element.21), channel_id=1, source_target_pairs={{0,16},{2,18},{4,20},{6,22},{8,24},{10,26},{12,28},{14,30},{16,0},... | collective-permute-start | bytes 1179656 | tf_op jit(solution)/shard_map/exchange_inputs/ppermute | solution.py:20
  10.9 58.8 %collective-permute-start.4 = (bf16[192,1024]{1,0:T(8,128)(2,1)}, bf16[192,1024]{1,0:T(8,128)(2,1)S(1)}, u32[]{:S(2)}, u32[]{:S(2)}) collective-permute-start(bf16[192,1024]{1,0:T(8,128)(2,1)} %get-tuple-element.18), channel_id=1, source_target_pairs={{0,16},{2,18},{4,20},{6,22},{8,24},{10,26},{12,28},{14,30},{16,0},... | collective-permute-start | bytes 1179656 | tf_op jit(solution)/shard_map/exchange_inputs/ppermute | solution.py:20
  11.0 60.2 %collective-permute-start.5 = (bf16[192,1024]{1,0:T(8,128)(2,1)}, bf16[192,1024]{1,0:T(8,128)(2,1)}, u32[]{:S(2)}, u32[]{:S(2)}) collective-permute-start(bf16[192,1024]{1,0:T(8,128)(2,1)} %get-tuple-element.19), channel_id=1, source_target_pairs={{0,16},{2,18},{4,20},{6,22},{8,24},{10,26},{12,28},{14,30},{16,0},... | collective-permute-start | bytes 1179656 | tf_op jit(solution)/shard_map/exchange_inputs/ppermute | solution.py:20
  39.5 28.3 %collective-permute-start.1 = (bf16[2,1,64,768]{3,2,0,1:T(8,128)(2,1)S(1)}, bf16[2,1,64,768]{3,2,0,1:T(8,128)(2,1)S(1)}, u32[]{:S(2)}, u32[]{:S(2)}) collective-permute-start(bf16[2,1,64,768]{3,2,0,1:T(8,128)(2,1)S(1)} %fusion.33), channel_id=1, source_target_pairs={{0,8},{2,10},{4,12},{6,14},{8,0},{10,2},{12,4},{14,6},{16,24},{18,... | collective-permute-start | bytes 589832 | tf_op jit(solution)/shard_map/gather_weight/ppermute | solution.py:20
  69.7 16.3 %collective-permute-start.6 = (bf16[192,1024]{1,0:T(8,128)(2,1)S(1)}, bf16[192,1024]{1,0:T(8,128)(2,1)S(1)}, u32[]{:S(2)}, u32[]{:S(2)}) collective-permute-start(bf16[192,1024]{1,0:T(8,128)(2,1)S(1)} %collective-permute-done.4), channel_id=1, source_target_pairs={{0,1},{1,0},{2,3},{3,2},{4,5},{5,4},{6,7},{7,6},{8,9},{9,8},{10,11... | collective-permute-start | bytes 1179656 | tf_op jit(solution)/shard_map/exchange_inputs/ppermute | solution.py:20
  71.2 17.7 %collective-permute-start.7 = (bf16[192,1024]{1,0:T(8,128)(2,1)}, bf16[192,1024]{1,0:T(8,128)(2,1)S(1)}, u32[]{:S(2)}, u32[]{:S(2)}) collective-permute-start(bf16[192,1024]{1,0:T(8,128)(2,1)} %collective-permute-done.5), channel_id=1, source_target_pairs={{0,1},{1,0},{2,3},{3,2},{4,5},{5,4},{6,7},{7,6},{8,9},{9,8},{10,11... | collective-permute-start | bytes 1179656 | tf_op jit(solution)/shard_map/exchange_inputs/ppermute | solution.py:20
  101.5 80.0 %collective-permute-start.12 = (bf16[64,768]{1,0:T(8,128)(2,1)S(1)}, bf16[64,768]{1,0:T(8,128)(2,1)S(1)}, u32[]{:S(2)}, u32[]{:S(2)}) collective-permute-start(bf16[64,768]{1,0:T(8,128)(2,1)S(1)} %bitcast.114), channel_id=1, source_target_pairs={{0,16},{2,18},{4,20},{6,22},{8,24},{10,26},{12,28},{14,30},{16,0},... | collective-permute-start | bytes 294920 | tf_op jit(solution)/shard_map/gather_other_weight/ppermute | solution.py:20
  161.4 58.2 %collective-permute-start.11 = (bf16[3,768,128]{2,1,0:T(8,128)(2,1)}, bf16[3,768,128]{2,1,0:T(8,128)(2,1)S(1)}, u32[]{:S(2)}, u32[]{:S(2)}) collective-permute-start(bf16[3,768,128]{2,1,0:T(8,128)(2,1)} %get-tuple-element.11), channel_id=1, source_target_pairs={{0,16},{2,18},{4,20},{6,22},{8,24},{10,26},{12,28},{14,30},{16,0},... | collective-permute-start | bytes 1769480 | tf_op jit(solution)/shard_map/return_grads/ppermute | solution.py:20
  164.3 50.3 %collective-permute-start.10 = (bf16[3,768,128]{2,1,0:T(8,128)(2,1)}, bf16[3,768,128]{2,1,0:T(8,128)(2,1)}, u32[]{:S(2)}, u32[]{:S(2)}) collective-permute-start(bf16[3,768,128]{2,1,0:T(8,128)(2,1)} %get-tuple-element.10), channel_id=1, source_target_pairs={{0,16},{2,18},{4,20},{6,22},{8,24},{10,26},{12,28},{14,30},{16,0},... | collective-permute-start | bytes 1769480 | tf_op jit(solution)/shard_map/return_grads/ppermute | solution.py:20
  180.9 35.1 %collective-permute-start.20 = (f32[2,4,64,384]{3,2,1,0:T(8,128)S(1)}, f32[2,4,64,384]{3,2,1,0:T(8,128)S(1)}, u32[]{:S(2)}, u32[]{:S(2)}) collective-permute-start(f32[2,4,64,384]{3,2,1,0:T(8,128)S(1)} %dynamic-slice_bitcast_fusion.1), channel_id=1, source_target_pairs={{0,2},{2,0},{4,6},{6,4},{8,10},{10,8},{12,14},{14,12},{16,18},{18,... | collective-permute-start | bytes 2359304 | tf_op jit(solution)/shard_map/weight_grad/ppermute | solution.py:20
  181.0 36.9 %collective-permute-start.23 = (f32[2,4,64,384]{3,2,1,0:T(8,128)S(1)}, f32[2,4,64,384]{3,2,1,0:T(8,128)S(1)}, u32[]{:S(2)}, u32[]{:S(2)}) collective-permute-start(f32[2,4,64,384]{3,2,1,0:T(8,128)S(1)} %dynamic-slice_bitcast_fusion), channel_id=1, source_target_pairs={{0,2},{2,0},{4,6},{6,4},{8,10},{10,8},{12,14},{14,12},{16,18},{18,... | collective-permute-start | bytes 2359304 | tf_op jit(solution)/shard_map/weight_grad/ppermute | solution.py:20
  192.7 23.0 %collective-permute-start.14 = (bf16[2,2,64,768]{3,2,1,0:T(8,128)(2,1)S(1)}, bf16[2,2,64,768]{3,2,1,0:T(8,128)(2,1)S(1)}, u32[]{:S(2)}, u32[]{:S(2)}) collective-permute-start(bf16[2,2,64,768]{3,2,1,0:T(8,128)(2,1)S(1)} %maximum_select_fusion.8), channel_id=1, source_target_pairs={{0,4},{2,6},{4,0},{6,2},{8,12},{10,14},{12,8},{14,10},{16,20},{18,... | collective-permute-start | bytes 1179656 | tf_op jit(solution)/shard_map/gather_other_weight/ppermute | solution.py:20
  215.9 21.0 %collective-permute-start.15 = (bf16[2,4,64,768]{3,2,1,0:T(8,128)(2,1)S(1)}, bf16[2,4,64,768]{3,2,1,0:T(8,128)(2,1)S(1)}, u32[]{:S(2)}, u32[]{:S(2)}) collective-permute-start(bf16[2,4,64,768]{3,2,1,0:T(8,128)(2,1)S(1)} %bitcast.90), channel_id=1, source_target_pairs={{0,2},{2,0},{4,6},{6,4},{8,10},{10,8},{12,14},{14,12},{16,18},{18,... | collective-permute-start | bytes 2359304 | tf_op jit(solution)/shard_map/gather_other_weight/ppermute | solution.py:20
  217.3 12.1 %collective-permute-start.21 = (f32[2,2,64,384]{3,2,1,0:T(8,128)S(1)}, f32[2,2,64,384]{3,2,1,0:T(8,128)S(1)}, u32[]{:S(2)}, u32[]{:S(2)}) collective-permute-start(f32[2,2,64,384]{3,2,1,0:T(8,128)S(1)} %dynamic-slice_bitcast_fusion.3), channel_id=1, source_target_pairs={{0,4},{2,6},{4,0},{6,2},{8,12},{10,14},{12,8},{14,10},{16,20},{18,... | collective-permute-start | bytes 1179656 | tf_op jit(solution)/shard_map/weight_grad/ppermute | solution.py:20
  218.0 18.2 %collective-permute-start.24 = (f32[2,2,64,384]{3,2,1,0:T(8,128)S(1)}, f32[2,2,64,384]{3,2,1,0:T(8,128)S(1)}, u32[]{:S(2)}, u32[]{:S(2)}) collective-permute-start(f32[2,2,64,384]{3,2,1,0:T(8,128)S(1)} %dynamic-slice_bitcast_fusion.2), channel_id=1, source_target_pairs={{0,4},{2,6},{4,0},{6,2},{8,12},{10,14},{12,8},{14,10},{16,20},{18,... | collective-permute-start | bytes 1179656 | tf_op jit(solution)/shard_map/weight_grad/ppermute | solution.py:20
  230.2 15.6 %collective-permute-start.22 = (f32[2,1,64,384]{3,2,1,0:T(8,128)}, f32[2,1,64,384]{3,2,1,0:T(8,128)}, u32[]{:S(2)}, u32[]{:S(2)}) collective-permute-start(f32[2,1,64,384]{3,2,1,0:T(8,128)} %constant_dynamic-slice_fusion.4), channel_id=1, source_target_pairs={{0,8},{2,10},{4,12},{6,14},{8,0},{10,2},{12,4},{14,6},{16,24},{18,... | collective-permute-start | bytes 589832 | tf_op jit(solution)/shard_map/weight_grad/ppermute | solution.py:20
  236.9 14.3 %collective-permute-start.25 = (f32[2,1,64,384]{3,2,1,0:T(8,128)}, f32[2,1,64,384]{3,2,1,0:T(8,128)}, u32[]{:S(2)}, u32[]{:S(2)}) collective-permute-start(f32[2,1,64,384]{3,2,1,0:T(8,128)} %constant_dynamic-slice_fusion.2), channel_id=1, source_target_pairs={{0,8},{2,10},{4,12},{6,14},{8,0},{10,2},{12,4},{14,6},{16,24},{18,... | collective-permute-start | bytes 589832 | tf_op jit(solution)/shard_map/weight_grad/ppermute | solution.py:20
  243.8 20.8 %collective-permute-start.16 = (f32[192,1024]{1,0:T(8,128)}, f32[192,1024]{1,0:T(8,128)}, u32[]{:S(2)}, u32[]{:S(2)}) collective-permute-start(f32[192,1024]{1,0:T(8,128)} %get-tuple-element.16), channel_id=1, source_target_pairs={{0,1},{1,0},{2,3},{3,2},{4,5},{5,4},{6,7},{7,6},{8,9},{9,8},{10,11... | collective-permute-start | bytes 2359304 | tf_op jit(solution)/shard_map/token_grad/ppermute | solution.py:20
  245.3 33.7 %collective-permute-start.17 = (f32[192,1024]{1,0:T(8,128)}, f32[192,1024]{1,0:T(8,128)}, u32[]{:S(2)}, u32[]{:S(2)}) collective-permute-start(f32[192,1024]{1,0:T(8,128)} %get-tuple-element.17), channel_id=1, source_target_pairs={{0,1},{1,0},{2,3},{3,2},{4,5},{5,4},{6,7},{7,6},{8,9},{9,8},{10,11... | collective-permute-start | bytes 2359304 | tf_op jit(solution)/shard_map/token_grad/ppermute | solution.py:20
  249.0 36.1 %collective-permute-start.26 = (f32[64,384]{1,0:T(8,128)}, f32[64,384]{1,0:T(8,128)}, u32[]{:S(2)}, u32[]{:S(2)}) collective-permute-start(f32[64,384]{1,0:T(8,128)} %get-tuple-element.25), channel_id=1, source_target_pairs={{0,16},{2,18},{4,20},{6,22},{8,24},{10,26},{12,28},{14,30},{16,0},... | collective-permute-start | bytes 294920 | tf_op jit(solution)/shard_map/weight_grad/ppermute | solution.py:20
  280.6 12.1 %collective-permute-start.18 = (bf16[192,1024]{1,0:T(8,128)(2,1)S(1)}, bf16[192,1024]{1,0:T(8,128)(2,1)S(1)}, u32[]{:S(2)}, u32[]{:S(2)}) collective-permute-start(bf16[192,1024]{1,0:T(8,128)(2,1)S(1)} %get-tuple-element.14), channel_id=1, source_target_pairs={{0,1},{1,0},{2,3},{3,2},{4,5},{5,4},{6,7},{7,6},{8,9},{9,8},{10,11... | collective-permute-start | bytes 1179656 | tf_op jit(solution)/shard_map/token_grad/ppermute | solution.py:20
  282.2 15.6 %collective-permute-start.19 = (bf16[192,1024]{1,0:T(8,128)(2,1)S(1)}, bf16[192,1024]{1,0:T(8,128)(2,1)S(1)}, u32[]{:S(2)}, u32[]{:S(2)}) collective-permute-start(bf16[192,1024]{1,0:T(8,128)(2,1)S(1)} %get-tuple-element.15), channel_id=1, source_target_pairs={{0,1},{1,0},{2,3},{3,2},{4,5},{5,4},{6,7},{7,6},{8,9},{9,8},{10,11... | collective-permute-start | bytes 1179656 | tf_op jit(solution)/shard_map/token_grad/ppermute | solution.py:20
  (26 other events, 310.1 us)

commit v2 on v1

v2 whole, which is shorter than its diff:
```python
import functools
import math

import jax
import jax.numpy as jnp
from jax import lax
from jax.experimental import pallas as pl
from jax.experimental.pallas import tpu as pltpu
from jax.sharding import PartitionSpec as P

F32 = jnp.float32
BF16 = jnp.bfloat16
LOG2E = math.log2(math.e)
PAIR = 128
TILE = 256


def flip(value, axis, mask):
    pairs = [(source, source ^ mask) for source in range(lax.axis_size(axis))]
    return lax.ppermute(value, axis, pairs)


def ordered(mine, other, bit):
    first = jnp.concatenate([mine, other], 0)
    second = jnp.concatenate([other, mine], 0)
    return jnp.where(bit == 0, first, second)


def attention_kernel(first, deps, *refs):
    slope_ref, q_ref, k_ref, v_ref, g_ref, logd_ref = refs[:6]
    rest = refs[6:]
    if first:
        dq_ref, dk_acc, dv_acc, kt_ref = rest[deps:]
    else:
        far_dq_ref, dk_in, dv_in = rest[:3]
        whole_ref, far_ref, dk_acc, dv_acc, kt_ref = rest[3 + deps :]
    step = pl.program_id(0)
    steps = pl.num_programs(0)
    size = PAIR // 2
    scale = size ** (-0.5)

    @pl.when(step == 0)
    def _():
        kt_ref[...] = k_ref[...].astype(F32).T.astype(BF16)
        if first:
            dk_acc[...] = jnp.zeros_like(dk_acc)
            dv_acc[...] = jnp.zeros_like(dv_acc)
        else:
            dk_acc[...] = dk_in[...]
            dv_acc[...] = dv_in[...]

    lane = lax.broadcasted_iota(jnp.int32, (TILE, PAIR), 1)
    key = k_ref[...]
    key_t = kt_ref[...]
    value = v_ref[...]
    query = q_ref[...].astype(F32)
    grad = g_ref[...].astype(F32)
    contract_last = (((1,), (1,)), ((), ()))
    grads_q = []
    for head in range(2):
        here = (lane >= head * size) & (lane < (head + 1) * size)
        q_head = jnp.where(here, query, 0.0).astype(BF16)
        g_head = jnp.where(here, grad, 0.0)
        g_scaled = (g_head * scale).astype(BF16)
        g_head = g_head.astype(BF16)
        score = lax.dot_general(key, q_head, contract_last, preferred_element_type=F32)
        score = score * (scale * LOG2E) - logd_ref[...] * slope_ref[head]
        top = jnp.max(score, axis=0, keepdims=True)
        expd = jnp.exp2(score - top)
        inverse = 1.0 / jnp.sum(expd, axis=0, keepdims=True)
        prob = expd * inverse
        prob_round = prob.astype(BF16)
        dprob = lax.dot_general(value, g_scaled, contract_last, preferred_element_type=F32)
        delta = jnp.sum(prob_round.astype(F32) * dprob, axis=0, keepdims=True)
        dscore = (prob * (dprob - delta)).astype(BF16)
        dv_acc[...] += jnp.dot(prob_round, g_head, preferred_element_type=F32)
        dk_acc[...] += jnp.dot(dscore, q_head, preferred_element_type=F32)
        grad_q = jnp.dot(key_t, dscore, preferred_element_type=F32)
        grads_q.append(grad_q[head * size : (head + 1) * size])
    grad_q = jnp.concatenate(grads_q, 0).T.astype(BF16)

    if first:
        dq_ref[...] = grad_q
        return

    whole_ref[pl.ds(pl.multiple_of(step * TILE, TILE), TILE), :PAIR] = grad_q

    @pl.when(step == steps - 1)
    def _():
        rows = far_ref.shape[0]
        dk = dk_acc[...].astype(BF16)
        dv = dv_acc[...].astype(BF16)
        whole_ref[rows:, :PAIR] = far_dq_ref[...]
        whole_ref[:, PAIR : 2 * PAIR] = dk
        whole_ref[:, 2 * PAIR :] = dv
        far_ref[:, :PAIR] = dk[rows:]
        far_ref[:, PAIR:] = dv[rows:]


def attention(first, pair, slopes, qkv, grad, logd, earlier, deps):
    both, _ = qkv.shape
    rows = both // 2
    steps = rows // TILE
    start = steps if first else 0
    acc = jax.ShapeDtypeStruct((both, PAIR), F32)
    fixed = lambda *shape: pl.BlockSpec(shape, lambda i: (0, 0))
    out_bf16 = lambda *shape: jax.ShapeDtypeStruct(shape, BF16)
    if first:
        out_shape = (out_bf16(rows, PAIR), acc, acc)
        out_specs = (pl.BlockSpec((TILE, PAIR), lambda i: (i, 0)), fixed(both, PAIR), fixed(both, PAIR))
        scratch = []
        earlier_specs = []
    else:
        out_shape = (out_bf16(both, 3 * PAIR), out_bf16(rows, 2 * PAIR))
        out_specs = (fixed(both, 3 * PAIR), fixed(rows, 2 * PAIR))
        scratch = [pltpu.VMEM((both, PAIR), F32), pltpu.VMEM((both, PAIR), F32)]
        earlier_specs = [fixed(rows, PAIR), fixed(both, PAIR), fixed(both, PAIR)]
    return pl.pallas_call(
        functools.partial(attention_kernel, first, len(deps)),
        grid=(steps,),
        out_shape=out_shape,
        in_specs=[
            pl.BlockSpec(memory_space=pltpu.SMEM),
            pl.BlockSpec((TILE, PAIR), lambda i: (start + i, 3 * pair)),
            pl.BlockSpec((both, PAIR), lambda i: (0, 3 * pair + 1)),
            pl.BlockSpec((both, PAIR), lambda i: (0, 3 * pair + 2)),
            pl.BlockSpec((TILE, PAIR), lambda i: (i, 0)),
            pl.BlockSpec((both, TILE), lambda i: (0, start + i)),
        ]
        + earlier_specs
        + [pl.BlockSpec(memory_space=pl.ANY)] * len(deps),
        out_specs=out_specs,
        scratch_shapes=scratch + [pltpu.VMEM((PAIR, both), BF16)],
        compiler_params=pltpu.CompilerParams(vmem_limit_bytes=48 * 2**20),
        cost_estimate=pl.CostEstimate(
            flops=24 * both * both * PAIR, bytes_accessed=16 * both * both, transcendentals=2 * both * both
        ),
    )(slopes[2 * pair : 2 * pair + 2], qkv, qkv, qkv, grad, logd, *earlier, *deps)


def on_device(tokens, qkv_weight, grad_attn, positions, slopes):
    rows, model = tokens.shape
    blocks = lax.axis_size("ctx")
    far_mask = blocks // 2
    bits = far_mask.bit_length() - 1
    me = lax.axis_index("ctx")
    side = me // far_mask
    head_side = lax.axis_index("head")
    shard, _, local_width = qkv_weight.shape
    width = local_width // 2
    heads = slopes.shape[0] // 2
    pairs = width // PAIR
    half_rows = rows // 2
    quarter = half_rows // 2

    def bit_of(position):
        return (me // 2**position) % 2

    def widen(stacked, position):
        arrived = flip(stacked, "ctx", 2**position)
        pieces = (stacked[:, :, None], arrived[:, :, None])
        along = [jnp.concatenate(c, 2) for c in (pieces, pieces[::-1])]
        stacked = jnp.where(bit_of(position) == 0, along[0], along[1])
        return stacked.reshape(2, -1, shard, 3 * width)

    with jax.named_scope("gather_weight"):
        weight_parts = []
        for which in (side, 1 - side):
            part = lax.dynamic_slice_in_dim(qkv_weight, which * width, width, 2)
            part = part.reshape(shard, 3, pairs, PAIR).transpose(0, 2, 1, 3)
            weight_parts.append(part.reshape(shard, 3 * width))
        far_positions = flip(positions, "ctx", far_mask)
        weight_far = flip(weight_parts[1], "ctx", far_mask)
        stacked = ordered(weight_parts[0][None], weight_far[None], side)[:, None]
        stacked, token_source = lax.optimization_barrier((stacked, tokens))
        for position in reversed(range(bits)):
            stacked = widen(stacked, position)
        weight = stacked.reshape(model, 3 * width)

    with jax.named_scope("exchange_inputs"):
        token_half = lax.dynamic_slice_in_dim(token_source, head_side * half_rows, half_rows, 0)
        near, cross = [], []
        for part in range(2):
            arrived = flip(token_half[part * quarter : (part + 1) * quarter], "ctx", far_mask)
            near.append(arrived)
            cross.append(flip(arrived, "head", 1))
        far_tokens = ordered(jnp.concatenate(near, 0), jnp.concatenate(cross, 0), head_side)
        grad_mine = lax.dynamic_slice_in_dim(grad_attn, side * width, width, 1)
        grad_theirs = lax.dynamic_slice_in_dim(grad_attn, (1 - side) * width, width, 1)
        first_theirs, _ = lax.optimization_barrier((grad_theirs[:, :PAIR], near[0]))
        grad_far = [flip(first_theirs, "ctx", far_mask)]
        slopes_mine = lax.dynamic_slice_in_dim(slopes, side * heads, heads, 0)

    with jax.named_scope("log_distance"):
        pos = jnp.concatenate([positions, far_positions], 0)
        logd = jnp.log(jnp.abs(pos[:, None] - pos[None, :]).astype(F32) + 1.0) * LOG2E

    with jax.named_scope("project"):
        qkv_own = jnp.dot(tokens, weight, preferred_element_type=F32).astype(BF16)
        qkv_far = jnp.dot(far_tokens, weight, preferred_element_type=F32).astype(BF16)
        qkv = jnp.concatenate([qkv_own, qkv_far], 0)
        both_tokens = jnp.concatenate([tokens, far_tokens], 0)

    late_mine, late_theirs, *late_grads = lax.optimization_barrier(
        (weight_parts[0], weight_parts[1], *[grad_theirs[:, p * PAIR : (p + 1) * PAIR] for p in range(1, pairs)], qkv_own)
    )[:-1]
    with jax.named_scope("exchange_inputs"):
        grad_far += [flip(g, "ctx", far_mask) for g in late_grads]
    with jax.named_scope("gather_other_weight"):
        back = flip(late_mine, "ctx", far_mask)
        stacked = ordered(late_theirs[None], back[None], side)[:, None]
    positions_left = list(reversed(range(bits)))

    def reduce_weight(total, position):
        bit = bit_of(position)
        folded = total.reshape(2, total.shape[1] // 2, 2, shard, total.shape[-1])
        send = lax.dynamic_index_in_dim(folded, 1 - bit, 2, keepdims=False)
        keep = lax.dynamic_index_in_dim(folded, bit, 2, keepdims=False)
        return keep + flip(send, "ctx", 2**position)

    deps = [stacked] + grad_far[1:]
    wholes, others, terms = [], [], []
    for pair in range(pairs):
        cut = slice(pair * PAIR, (pair + 1) * PAIR)
        with jax.named_scope("attention_far_queries"):
            far_dq, *sums = attention(
                True, pair, slopes_mine, qkv, grad_far[pair], logd, [], deps if pair else []
            )
        if pair:
            deps = [other_rest]
        with jax.named_scope("return_grads"):
            other_dq = flip(far_dq, "ctx", far_mask)
        if positions_left and pair:
            with jax.named_scope("gather_other_weight"):
                stacked = widen(stacked, positions_left.pop(0))
            with jax.named_scope("weight_grad"):
                terms[0] = reduce_weight(terms[0], 0)
            deps += [stacked, terms[0]]
        with jax.named_scope("attention_own_queries"):
            whole, far_rest = attention(
                False, pair, slopes_mine, qkv, grad_mine[:, cut], logd, [far_dq, *sums], deps
            )
        deps = [other_dq]
        if positions_left and not pair:
            with jax.named_scope("gather_other_weight"):
                stacked = widen(stacked, positions_left.pop(0))
                deps.append(stacked)
        with jax.named_scope("return_grads"):
            other_rest = flip(far_rest, "ctx", far_mask)
        wholes.append(whole)
        others.append(jnp.concatenate([other_dq, other_rest], 1))
        with jax.named_scope("weight_grad"):
            term = lax.dot_general(both_tokens, whole, (((0,), (0,)), ((), ())), preferred_element_type=F32)
            terms.append(term.reshape(2, far_mask, shard, 3 * PAIR))

    with jax.named_scope("gather_other_weight"):
        for position in positions_left:
            stacked = widen(stacked, position)
        weight_other = stacked.reshape(model, 3 * width)

    with jax.named_scope("weight_grad"):
        kept, arrived = [], []
        for pair, total in enumerate(terms):
            for position in range(0 if pair else 1, bits):
                total = reduce_weight(total, position)
            total = total.reshape(2, shard, 3 * PAIR)
            kept.append(lax.dynamic_index_in_dim(total, side, 0, keepdims=False))
            arrived.append(flip(lax.dynamic_index_in_dim(total, 1 - side, 0, keepdims=False), "ctx", far_mask))
        kept, arrived = [
            jnp.stack([t.reshape(shard, 3, PAIR) for t in side_terms], 2).reshape(shard, 3, width)
            for side_terms in (kept, arrived)
        ]
        d_weight = jnp.where(
            side == 0, jnp.concatenate([kept, arrived], 2), jnp.concatenate([arrived, kept], 2)
        )

    with jax.named_scope("token_grad"):
        dqkv = jnp.concatenate([w[:rows] for w in wholes] + others, 1)
        joined = jnp.concatenate([weight, weight_other], 1)

        def partial_rows(part):
            rows_part = lax.dynamic_slice_in_dim(dqkv, part * half_rows, half_rows, 0)
            return lax.dot_general(rows_part, joined, (((1,), (1,)), ((), ())), preferred_element_type=F32)

        sent = partial_rows(1 - head_side)
        kept = partial_rows(head_side)
        mine, cross = [], []
        for part in range(2):
            cut = slice(part * quarter, (part + 1) * quarter)
            total = (kept[cut] + flip(sent[cut], "head", 1)).astype(BF16)
            mine.append(total)
            cross.append(flip(total, "head", 1))
        d_tokens = ordered(jnp.concatenate(mine, 0), jnp.concatenate(cross, 0), head_side)
    return (d_tokens, d_weight)


def solution(mesh):
    placed = (P("ctx", None), P("ctx", None, "head"), P("ctx", "head"), P("ctx"), P("head"))
    return jax.shard_map(
        on_device,
        mesh=mesh,
        in_specs=placed,
        out_specs=(P("ctx", None), P("ctx", None, "head")),
        check_vma=False,
    )
```

time: 300 us -> 231 us (0.77)
  waiting for transfers between devices: 144 us -> 106 us
  local copies, waits for them, and re-layouts: 36.7 us -> 8.57 us
  matrix products: 15.1 us -> 9.28 us
    ppermute x28 -> x31, waiting for transfers between devices: 144 us -> 106 us  [flip(): return lax.ppermute(value, axis, pairs)]
    unnamed x49 -> x24, local copies, waits for them, and re-layouts: 7.27 us -> 1.17 us
    dot_general x4, matrix products: 12.3 us -> 6.49 us  [the longest x2 3.68 us: on_device(): lax.dot_general(both_tokens, whole, (((0,), (0,)), ((), ())), preferred_e...]
    reshape x10, local copies, waits for them, and re-layouts: 6.46 us -> 0.71 us  [the longest x6 0.48 us: on_device(): jnp.stack([t.reshape(shard, 3, PAIR) for t in side_terms], 2)]
    transpose x3 -> x2, local copies, waits for them, and re-layouts: 5.33 us -> 0.17 us  [on_device(): part = part.reshape(shard, 3, pairs, PAIR).transpose(0, 2, 1, 3)]
    select_n x6 -> x4, local copies, waits for them, and re-layouts: 5.1 us -> 0.35 us  [widen(): stacked = jnp.where(bit_of(position) == 0, along[0], along[1])]
    dot_general x2 -> x0, local copies, waits for them, and re-layouts: 3.57 us -> none  [on_device(): jnp.einsum('sd,csf->dcf', both_tokens, stacked, preferred_element_type=F32)]
    squeeze x6, local copies, waits for them, and re-layouts: 4.04 us -> 0.98 us  [reduce_weight(): send = lax.dynamic_index_in_dim(folded, 1 - bit, 2, keepdims=False)]
  transfers between devices with their start and end apart: 28 -> 31, of which waited for: 13 -> 14; matrix products, arithmetic and copies ran while one was open for 18% -> 13% of each run, Pallas kernels for 18% -> 25%
where the time goes in v2:
time: 231 us; the launch traced here: 230 us
  waiting for transfers between devices  106 us (46%)
  Pallas kernels  56.9 us (25%)
  starting transfers between devices  32.4 us (14%)
  other arithmetic  16.1 us (7%)
  matrix products  9.28 us (4%)
  local copies, waits for them, and re-layouts  8.57 us (4%)
    ppermute x31, waiting for transfers between devices, flip(): return lax.ppermute(value, axis, pairs)  106 us
    pallas_call x4, Pallas kernels, attention(): pl.pallas_call(functools.partial(attention_kernel, first, len(deps)), gri...  56.9 us
    ppermute x31, starting transfers between devices, flip(): return lax.ppermute(value, axis, pairs)  32.4 us
    mul x1, other arithmetic, on_device(): jnp.log(jnp.abs(pos[:, None] - pos[None, :]).astype(F32) + 1.0) * LOG2E  5.57 us
  transfers between devices with their start and end apart: 31, of which 14 were waited for; matrix products, arithmetic and copies ran while one was open for 13% of the time, Pallas kernels for 25%

profile of v2, /device:TPU:0, one launch (start us, length us, event | category | flops | bytes accessed | tf_op | source)
XLA Modules:
  0.0 230.3 jit_solution(13562552829737924886)
XLA Ops:
  2.0 4.1 %collective-permute-start = (bf16[64,768]{1,0:T(8,128)(2,1)S(1)}, bf16[64,768]{1,0:T(8,128)(2,1)S(1)}, u32[]{:S(2)}, u32[]{:S(2)}) collective-permute-start(bf16[64,768]{1,0:T(8,128)(2,1)S(1)} %reshape.495), channel_id=1, source_target_pairs={{0,16},{2,18},{4,20},{6,22},{8,24},{10,26},{12,28},{14,30},{16,0},... | collective-permute-start | bytes 294920 | tf_op jit(solution)/shard_map/gather_weight/ppermute | solution.py:20
  6.5 4.6 %collective-permute-done = bf16[64,768]{1,0:T(8,128)(2,1)S(1)} collective-permute-done((bf16[64,768]{1,0:T(8,128)(2,1)S(1)}, bf16[64,768]{1,0:T(8,128)(2,1)S(1)}, u32[]{:S(2)}, u32[]{:S(2)}) %collective-permute-start) | collective-permute-done | bytes 98336 | tf_op jit(solution)/shard_map/gather_weight/ppermute | solution.py:20
  13.0 3.3 %collective-permute-start.4 = (bf16[192,1024]{1,0:T(8,128)(2,1)}, bf16[192,1024]{1,0:T(8,128)(2,1)}, u32[]{:S(2)}, u32[]{:S(2)}) collective-permute-start(bf16[192,1024]{1,0:T(8,128)(2,1)} %get-tuple-element.38), channel_id=1, source_target_pairs={{0,16},{2,18},{4,20},{6,22},{8,24},{10,26},{12,28},{14,30},{16,0},... | collective-permute-start | bytes 1179656 | tf_op jit(solution)/shard_map/exchange_inputs/ppermute | solution.py:20
  20.4 23.0 %collective-permute-done.4 = bf16[192,1024]{1,0:T(8,128)(2,1)} collective-permute-done((bf16[192,1024]{1,0:T(8,128)(2,1)}, bf16[192,1024]{1,0:T(8,128)(2,1)}, u32[]{:S(2)}, u32[]{:S(2)}) %collective-permute-start.4) | collective-permute-done | bytes 393248 | tf_op jit(solution)/shard_map/exchange_inputs/ppermute | solution.py:20
  45.0 5.9 %collective-permute-done.5 = bf16[192,1024]{1,0:T(8,128)(2,1)} collective-permute-done((bf16[192,1024]{1,0:T(8,128)(2,1)}, bf16[192,1024]{1,0:T(8,128)(2,1)}, u32[]{:S(2)}, u32[]{:S(2)}) %collective-permute-start.5) | collective-permute-done | bytes 393248 | tf_op jit(solution)/shard_map/exchange_inputs/ppermute | solution.py:20
  53.8 5.6 %log_multiply_fusion.refs_5_ = f32[1536,1536]{1,0:T(8,128)} fusion(s32[1536]{0:T(1024)S(1)} %constant_dynamic-update-slice_fusion.5), kind=kLoop, calls=%fused_computation | loop fusion | flops 11796480 | bytes 9443328 | tf_op jit(solution)/shard_map/log_distance/mul | solution.py:196
  59.4 1.9 collective-permute-done.7
  67.4 1.9 collective-permute-start.11
  69.4 8.5 %collective-permute-done.9.refs_4_ = bf16[768,128]{1,0:T(8,128)(2,1)S(1)} collective-permute-done((bf16[768,128]{1,0:T(8,128)(2,1)S(1)}, bf16[768,128]{1,0:T(8,128)(2,1)S(1)}, u32[]{:S(2)}, u32[]{:S(2)}) %collective-permute-start.9) | collective-permute-done | bytes 196640 | tf_op jit(solution)/shard_map/exchange_inputs/ppermute | solution.py:20
  77.9 14.0 %attention_far_queries.2 = (bf16[768,128]{1,0:T(8,128)(2,1)S(1)}, f32[1536,128]{1,0:T(8,128)S(1)}, f32[1536,128]{1,0:T(8,128)S(1)}) custom-call(f32[2]{0:T(128)S(1)} %get-tuple-element.53.refs_0_, bf16[1536,768]{1,0:T(8,128)(2,1)S(1)} %pad_maximum_fusion.2.refs_1_.refs_2_.refs_3_, bf16[1536,768]{1,0:T(8,128)(2,1)S(1)} %pad_maximum_fusion.2.refs_1_.refs_2_.refs_3_, ...), custom_call_target="tpu_custom_call" | custom-call | flops 7247757312 | bytes 37748736 | tf_op jit(solution)/shard_map/attention_far_queries/pallas_call | solution.py:118
  92.1 2.0 collective-permute-start.13
  94.2 14.5 %attention_own_queries.2 = (bf16[1536,384]{1,0:T(8,128)(2,1)S(1)}, bf16[768,256]{1,0:T(8,128)(2,1)S(1)}) custom-call(f32[2]{0:T(128)S(1)} %get-tuple-element.53.refs_0_, bf16[1536,768]{1,0:T(8,128)(2,1)} %copy-done, bf16[1536,768]{1,0:T(8,128)(2,1)} %copy-done, bf16[1536,768]{1,0:T(8,128)(2,1)} %copy-done, bf16[768,128]{1,0:T(8,128)(2,1)S(1)} %get-tuple-element.42.refs_4_, ...), custom_call_target="tpu_custom_call" | custom-call | flops 7247757312 | bytes 37748736 | tf_op jit(solution)/shard_map/attention_own_queries/pallas_call | solution.py:118
  114.3 14.0 %attention_far_queries.3 = (bf16[768,128]{1,0:T(8,128)(2,1)S(1)}, f32[1536,128]{1,0:T(8,128)S(1)}, f32[1536,128]{1,0:T(8,128)S(1)}) custom-call(f32[2]{0:T(128)S(1)} %get-tuple-element.52.refs_0_, bf16[1536,768]{1,0:T(8,128)(2,1)S(1)} %copy-done.1, bf16[1536,768]{1,0:T(8,128)(2,1)S(1)} %copy-done.1, bf16[1536,768]{1,0:T(8,128)(2,1)S(1)} %copy-done.1, ...), custom_call_target="tpu_custom_call" | custom-call | flops 7247757312 | bytes 37748736 | tf_op jit(solution)/shard_map/attention_far_queries/pallas_call | solution.py:118
  128.4 2.0 collective-permute-start.17
  131.5 14.3 %attention_own_queries.3 = (bf16[1536,384]{1,0:T(8,128)(2,1)S(1)}, bf16[768,256]{1,0:T(8,128)(2,1)S(1)}) custom-call(f32[2]{0:T(128)S(1)} %get-tuple-element.52.refs_0_, bf16[1536,768]{1,0:T(8,128)(2,1)} %copy-done, bf16[1536,768]{1,0:T(8,128)(2,1)} %copy-done, bf16[1536,768]{1,0:T(8,128)(2,1)} %copy-done, bf16[768,128]{1,0:T(8,128)(2,1)S(1)} %get-tuple-element.40.refs_4_, ...), custom_call_target="tpu_custom_call" | custom-call | flops 7247757312 | bytes 37748736 | tf_op jit(solution)/shard_map/attention_own_queries/pallas_call | solution.py:118
  149.5 2.1 collective-permute-start.25
  151.6 17.1 %collective-permute-done.18 = bf16[768,256]{1,0:T(8,128)(2,1)S(1)} collective-permute-done((bf16[768,256]{1,0:T(8,128)(2,1)S(1)}, bf16[768,256]{1,0:T(8,128)(2,1)S(1)}, u32[]{:S(2)}, u32[]{:S(2)}) %collective-permute-start.18) | collective-permute-done | bytes 393248 | tf_op jit(solution)/shard_map/return_grads/ppermute | solution.py:20
  178.0 5.1 %collective-permute-done.29 = f32[64,384]{1,0:T(8,128)S(1)} collective-permute-done((f32[64,384]{1,0:T(8,128)}, f32[64,384]{1,0:T(8,128)S(1)}, u32[]{:S(2)}, u32[]{:S(2)}) %collective-permute-start.29) | collective-permute-done | bytes 98336 | tf_op jit(solution)/shard_map/weight_grad/ppermute | solution.py:20
  183.2 2.1 collective-permute-done.27
  186.4 5.8 %collective-permute-done.20 = f32[192,1024]{1,0:T(8,128)} collective-permute-done((f32[192,1024]{1,0:T(8,128)}, f32[192,1024]{1,0:T(8,128)}, u32[]{:S(2)}, u32[]{:S(2)}) %collective-permute-start.20) | collective-permute-done | bytes 786464 | tf_op jit(solution)/shard_map/token_grad/ppermute | solution.py:20
  192.2 15.9 %collective-permute-done.21 = f32[192,1024]{1,0:T(8,128)} collective-permute-done((f32[192,1024]{1,0:T(8,128)S(1)}, f32[192,1024]{1,0:T(8,128)}, u32[]{:S(2)}, u32[]{:S(2)}) %collective-permute-start.21) | collective-permute-done | bytes 786464 | tf_op jit(solution)/shard_map/token_grad/ppermute | solution.py:20
  212.6 5.3 %collective-permute-done.30 = f32[64,384]{1,0:T(8,128)S(1)} collective-permute-done((f32[64,384]{1,0:T(8,128)S(1)}, f32[64,384]{1,0:T(8,128)S(1)}, u32[]{:S(2)}, u32[]{:S(2)}) %collective-permute-start.30) | collective-permute-done | bytes 98336 | tf_op jit(solution)/shard_map/weight_grad/ppermute | solution.py:20
  219.1 2.9 %collective-permute-done.22 = bf16[192,1024]{1,0:T(8,128)(2,1)S(1)} collective-permute-done((bf16[192,1024]{1,0:T(8,128)(2,1)S(1)}, bf16[192,1024]{1,0:T(8,128)(2,1)S(1)}, u32[]{:S(2)}, u32[]{:S(2)}) %collective-permute-start.22) | collective-permute-done | bytes 393248 | tf_op jit(solution)/shard_map/token_grad/ppermute | solution.py:20
  222.0 6.6 %collective-permute-done.23 = bf16[192,1024]{1,0:T(8,128)(2,1)S(1)} collective-permute-done((bf16[192,1024]{1,0:T(8,128)(2,1)S(1)}, bf16[192,1024]{1,0:T(8,128)(2,1)S(1)}, u32[]{:S(2)}, u32[]{:S(2)}) %collective-permute-start.23) | collective-permute-done | bytes 393248 | tf_op jit(solution)/shard_map/token_grad/ppermute | solution.py:20
  (135 shorter events, 46.2 us)
Async XLA Ops:
  6.1 14.2 %collective-permute-start.8 = (s32[768]{0:T(1024)}, s32[768]{0:T(1024)S(1)}, u32[]{:S(2)}, u32[]{:S(2)}) collective-permute-start(s32[768]{0:T(1024)} %param.8), channel_id=1, source_target_pairs={{0,16},{2,18},{4,20},{6,22},{8,24},{10,26},{12,28},{14,30},{16,0},... | collective-permute-start | bytes 9224 | tf_op jit(solution)/shard_map/gather_weight/ppermute | solution.py:20
  13.0 30.5 %collective-permute-start.4 = (bf16[192,1024]{1,0:T(8,128)(2,1)}, bf16[192,1024]{1,0:T(8,128)(2,1)}, u32[]{:S(2)}, u32[]{:S(2)}) collective-permute-start(bf16[192,1024]{1,0:T(8,128)(2,1)} %get-tuple-element.38), channel_id=1, source_target_pairs={{0,16},{2,18},{4,20},{6,22},{8,24},{10,26},{12,28},{14,30},{16,0},... | collective-permute-start | bytes 1179656 | tf_op jit(solution)/shard_map/exchange_inputs/ppermute | solution.py:20
  16.3 34.6 %collective-permute-start.5 = (bf16[192,1024]{1,0:T(8,128)(2,1)}, bf16[192,1024]{1,0:T(8,128)(2,1)}, u32[]{:S(2)}, u32[]{:S(2)}) collective-permute-start(bf16[192,1024]{1,0:T(8,128)(2,1)} %get-tuple-element.39), channel_id=1, source_target_pairs={{0,16},{2,18},{4,20},{6,22},{8,24},{10,26},{12,28},{14,30},{16,0},... | collective-permute-start | bytes 1179656 | tf_op jit(solution)/shard_map/exchange_inputs/ppermute | solution.py:20
  18.0 34.4 %collective-permute-start.2 = (bf16[2,2,64,768]{3,2,0,1:T(8,128)(2,1)}, bf16[2,2,64,768]{3,2,0,1:T(8,128)(2,1)}, u32[]{:S(2)}, u32[]{:S(2)}) collective-permute-start(bf16[2,2,64,768]{3,2,0,1:T(8,128)(2,1)} %maximum_select_fusion.7), channel_id=1, source_target_pairs={{0,4},{2,6},{4,0},{6,2},{8,12},{10,14},{12,8},{14,10},{16,20},{18,... | collective-permute-start | bytes 1179656 | tf_op jit(solution)/shard_map/gather_weight/ppermute | solution.py:20
  43.4 16.0 %collective-permute-start.6 = (bf16[192,1024]{1,0:T(8,128)(2,1)}, bf16[192,1024]{1,0:T(8,128)(2,1)S(1)}, u32[]{:S(2)}, u32[]{:S(2)}) collective-permute-start(bf16[192,1024]{1,0:T(8,128)(2,1)} %collective-permute-done.4), channel_id=1, source_target_pairs={{0,1},{1,0},{2,3},{3,2},{4,5},{5,4},{6,7},{7,6},{8,9},{9,8},{10,11... | collective-permute-start | bytes 1179656 | tf_op jit(solution)/shard_map/exchange_inputs/ppermute | solution.py:20
  59.4 18.5 %collective-permute-start.9 = (bf16[768,128]{1,0:T(8,128)(2,1)S(1)}, bf16[768,128]{1,0:T(8,128)(2,1)S(1)}, u32[]{:S(2)}, u32[]{:S(2)}) collective-permute-start(bf16[768,128]{1,0:T(8,128)(2,1)S(1)} %copy-done.5), channel_id=1, source_target_pairs={{0,16},{2,18},{4,20},{6,22},{8,24},{10,26},{12,28},{14,30},{16,0},... | collective-permute-start | bytes 589832 | tf_op jit(solution)/shard_map/exchange_inputs/ppermute | solution.py:20
  66.2 25.8 %collective-permute-start.10 = (bf16[64,768]{1,0:T(8,128)(2,1)S(1)}, bf16[64,768]{1,0:T(8,128)(2,1)S(1)}, u32[]{:S(2)}, u32[]{:S(2)}) collective-permute-start(bf16[64,768]{1,0:T(8,128)(2,1)S(1)} %reshape.496), channel_id=1, source_target_pairs={{0,16},{2,18},{4,20},{6,22},{8,24},{10,26},{12,28},{14,30},{16,0},... | collective-permute-start | bytes 294920 | tf_op jit(solution)/shard_map/gather_other_weight/ppermute | solution.py:20
  67.4 26.8 %collective-permute-start.11 = (bf16[768,128]{1,0:T(8,128)(2,1)S(1)}, bf16[768,128]{1,0:T(8,128)(2,1)S(1)}, u32[]{:S(2)}, u32[]{:S(2)}) collective-permute-start(bf16[768,128]{1,0:T(8,128)(2,1)S(1)} %copy-done.4), channel_id=1, source_target_pairs={{0,16},{2,18},{4,20},{6,22},{8,24},{10,26},{12,28},{14,30},{16,0},... | collective-permute-start | bytes 589832 | tf_op jit(solution)/shard_map/exchange_inputs/ppermute | solution.py:20
  92.0 22.3 %collective-permute-start.12 = (bf16[768,128]{1,0:T(8,128)(2,1)S(1)}, bf16[768,128]{1,0:T(8,128)(2,1)S(1)}, u32[]{:S(2)}, u32[]{:S(2)}) collective-permute-start(bf16[768,128]{1,0:T(8,128)(2,1)S(1)} %get-tuple-element.21.refs_6_), channel_id=1, source_target_pairs={{0,16},{2,18},{4,20},{6,22},{8,24},{10,26},{12,28},{14,30},{16,0},... | collective-permute-start | bytes 589832 | tf_op jit(solution)/shard_map/return_grads/ppermute | solution.py:20
  92.1 20.6 %collective-permute-start.13 = (bf16[2,1,64,768]{3,2,0,1:T(8,128)(2,1)S(1)}, bf16[2,1,64,768]{3,2,0,1:T(8,128)(2,1)S(1)}, u32[]{:S(2)}, u32[]{:S(2)}) collective-permute-start(bf16[2,1,64,768]{3,2,0,1:T(8,128)(2,1)S(1)} %maximum_select_fusion.11), channel_id=1, source_target_pairs={{0,8},{2,10},{4,12},{6,14},{8,0},{10,2},{12,4},{14,6},{16,24},{18,... | collective-permute-start | bytes 589832 | tf_op jit(solution)/shard_map/gather_other_weight/ppermute | solution.py:20
  110.6 20.1 %collective-permute-start.16 = (f32[2,4,64,384]{3,2,1,0:T(8,128)S(1)}, f32[2,4,64,384]{3,2,1,0:T(8,128)S(1)}, u32[]{:S(2)}, u32[]{:S(2)}) collective-permute-start(f32[2,4,64,384]{3,2,1,0:T(8,128)S(1)} %dynamic-slice_bitcast_fusion.1), channel_id=1, source_target_pairs={{0,2},{2,0},{4,6},{6,4},{8,10},{10,8},{12,14},{14,12},{16,18},{18,... | collective-permute-start | bytes 2359304 | tf_op jit(solution)/shard_map/weight_grad/ppermute | solution.py:20
  110.7 20.8 %collective-permute-start.14 = (bf16[768,256]{1,0:T(8,128)(2,1)S(1)}, bf16[768,256]{1,0:T(8,128)(2,1)S(1)}, u32[]{:S(2)}, u32[]{:S(2)}) collective-permute-start(bf16[768,256]{1,0:T(8,128)(2,1)S(1)} %get-tuple-element.31), channel_id=1, source_target_pairs={{0,16},{2,18},{4,20},{6,22},{8,24},{10,26},{12,28},{14,30},{16,0},... | collective-permute-start | bytes 1179656 | tf_op jit(solution)/shard_map/return_grads/ppermute | solution.py:20
  112.8 17.7 %collective-permute-start.15 = (bf16[2,2,64,768]{3,2,1,0:T(8,128)(2,1)S(1)}, bf16[2,2,64,768]{3,2,1,0:T(8,128)(2,1)S(1)}, u32[]{:S(2)}, u32[]{:S(2)}) collective-permute-start(bf16[2,2,64,768]{3,2,1,0:T(8,128)(2,1)S(1)} %copy_select_fusion.refs_7_), channel_id=1, source_target_pairs={{0,4},{2,6},{4,0},{6,2},{8,12},{10,14},{12,8},{14,10},{16,20},{18,... | collective-permute-start | bytes 1179656 | tf_op jit(solution)/shard_map/gather_other_weight/ppermute | solution.py:20
  128.4 21.0 %collective-permute-start.17 = (bf16[768,128]{1,0:T(8,128)(2,1)S(1)}, bf16[768,128]{1,0:T(8,128)(2,1)S(1)}, u32[]{:S(2)}, u32[]{:S(2)}) collective-permute-start(bf16[768,128]{1,0:T(8,128)(2,1)S(1)} %get-tuple-element.28.refs_6_), channel_id=1, source_target_pairs={{0,16},{2,18},{4,20},{6,22},{8,24},{10,26},{12,28},{14,30},{16,0},... | collective-permute-start | bytes 589832 | tf_op jit(solution)/shard_map/return_grads/ppermute | solution.py:20
  130.6 38.1 %collective-permute-start.19 = (bf16[2,4,64,768]{3,2,1,0:T(8,128)(2,1)S(1)}, bf16[2,4,64,768]{3,2,1,0:T(8,128)(2,1)S(1)}, u32[]{:S(2)}, u32[]{:S(2)}) collective-permute-start(bf16[2,4,64,768]{3,2,1,0:T(8,128)(2,1)S(1)} %bitcast.74), channel_id=1, source_target_pairs={{0,2},{2,0},{4,6},{6,4},{8,10},{10,8},{12,14},{14,12},{16,18},{18,... | collective-permute-start | bytes 2359304 | tf_op jit(solution)/shard_map/gather_other_weight/ppermute | solution.py:20
  130.9 18.5 %collective-permute-start.24 = (f32[2,2,64,384]{3,2,1,0:T(8,128)S(1)}, f32[2,2,64,384]{3,2,1,0:T(8,128)S(1)}, u32[]{:S(2)}, u32[]{:S(2)}) collective-permute-start(f32[2,2,64,384]{3,2,1,0:T(8,128)S(1)} %dynamic-slice_bitcast_fusion.3), channel_id=1, source_target_pairs={{0,4},{2,6},{4,0},{6,2},{8,12},{10,14},{12,8},{14,10},{16,20},{18,... | collective-permute-start | bytes 1179656 | tf_op jit(solution)/shard_map/weight_grad/ppermute | solution.py:20
  147.7 25.8 %collective-permute-start.26 = (f32[2,4,64,384]{3,2,1,0:T(8,128)S(1)}, f32[2,4,64,384]{3,2,1,0:T(8,128)S(1)}, u32[]{:S(2)}, u32[]{:S(2)}) collective-permute-start(f32[2,4,64,384]{3,2,1,0:T(8,128)S(1)} %dynamic-slice_bitcast_fusion), channel_id=1, source_target_pairs={{0,2},{2,0},{4,6},{6,4},{8,10},{10,8},{12,14},{14,12},{16,18},{18,... | collective-permute-start | bytes 2359304 | tf_op jit(solution)/shard_map/weight_grad/ppermute | solution.py:20
  148.2 20.5 %collective-permute-start.18 = (bf16[768,256]{1,0:T(8,128)(2,1)S(1)}, bf16[768,256]{1,0:T(8,128)(2,1)S(1)}, u32[]{:S(2)}, u32[]{:S(2)}) collective-permute-start(bf16[768,256]{1,0:T(8,128)(2,1)S(1)} %get-tuple-element.33), channel_id=1, source_target_pairs={{0,16},{2,18},{4,20},{6,22},{8,24},{10,26},{12,28},{14,30},{16,0},... | collective-permute-start | bytes 1179656 | tf_op jit(solution)/shard_map/return_grads/ppermute | solution.py:20
  149.5 26.4 %collective-permute-start.25 = (f32[2,1,64,384]{3,2,1,0:T(8,128)S(1)}, f32[2,1,64,384]{3,2,1,0:T(8,128)S(1)}, u32[]{:S(2)}, u32[]{:S(2)}) collective-permute-start(f32[2,1,64,384]{3,2,1,0:T(8,128)S(1)} %constant_dynamic-slice_fusion.6), channel_id=1, source_target_pairs={{0,8},{2,10},{4,12},{6,14},{8,0},{10,2},{12,4},{14,6},{16,24},{18,... | collective-permute-start | bytes 589832 | tf_op jit(solution)/shard_map/weight_grad/ppermute | solution.py:20
  171.5 20.7 %collective-permute-start.20 = (f32[192,1024]{1,0:T(8,128)}, f32[192,1024]{1,0:T(8,128)}, u32[]{:S(2)}, u32[]{:S(2)}) collective-permute-start(f32[192,1024]{1,0:T(8,128)} %get-tuple-element.36), channel_id=1, source_target_pairs={{0,1},{1,0},{2,3},{3,2},{4,5},{5,4},{6,7},{7,6},{8,9},{9,8},{10,11... | collective-permute-start | bytes 2359304 | tf_op jit(solution)/shard_map/token_grad/ppermute | solution.py:20
  172.0 36.2 %collective-permute-start.21 = (f32[192,1024]{1,0:T(8,128)S(1)}, f32[192,1024]{1,0:T(8,128)}, u32[]{:S(2)}, u32[]{:S(2)}) collective-permute-start(f32[192,1024]{1,0:T(8,128)S(1)} %get-tuple-element.37), channel_id=1, source_target_pairs={{0,1},{1,0},{2,3},{3,2},{4,5},{5,4},{6,7},{7,6},{8,9},{9,8},{10,11... | collective-permute-start | bytes 2359304 | tf_op jit(solution)/shard_map/token_grad/ppermute | solution.py:20
  186.4 25.6 %collective-permute-start.28 = (f32[2,1,64,384]{3,2,1,0:T(8,128)S(1)}, f32[2,1,64,384]{3,2,1,0:T(8,128)S(1)}, u32[]{:S(2)}, u32[]{:S(2)}) collective-permute-start(f32[2,1,64,384]{3,2,1,0:T(8,128)S(1)} %constant_dynamic-slice_fusion.4), channel_id=1, source_target_pairs={{0,8},{2,10},{4,12},{6,14},{8,0},{10,2},{12,4},{14,6},{16,24},{18,... | collective-permute-start | bytes 589832 | tf_op jit(solution)/shard_map/weight_grad/ppermute | solution.py:20
  209.9 12.1 %collective-permute-start.22 = (bf16[192,1024]{1,0:T(8,128)(2,1)S(1)}, bf16[192,1024]{1,0:T(8,128)(2,1)S(1)}, u32[]{:S(2)}, u32[]{:S(2)}) collective-permute-start(bf16[192,1024]{1,0:T(8,128)(2,1)S(1)} %get-tuple-element.34), channel_id=1, source_target_pairs={{0,1},{1,0},{2,3},{3,2},{4,5},{5,4},{6,7},{7,6},{8,9},{9,8},{10,11... | collective-permute-start | bytes 1179656 | tf_op jit(solution)/shard_map/token_grad/ppermute | solution.py:20
  210.4 18.1 %collective-permute-start.23 = (bf16[192,1024]{1,0:T(8,128)(2,1)S(1)}, bf16[192,1024]{1,0:T(8,128)(2,1)S(1)}, u32[]{:S(2)}, u32[]{:S(2)}) collective-permute-start(bf16[192,1024]{1,0:T(8,128)(2,1)S(1)} %get-tuple-element.35), channel_id=1, source_target_pairs={{0,1},{1,0},{2,3},{3,2},{4,5},{5,4},{6,7},{7,6},{8,9},{9,8},{10,11... | collective-permute-start | bytes 1179656 | tf_op jit(solution)/shard_map/token_grad/ppermute | solution.py:20
  (16 other events, 132.0 us)

commit v3 on v2

--- a/solution.py
+++ b/solution.py
@@ -18,6 +18,10 @@
 def flip(value, axis, mask):
     pairs = [(source, source ^ mask) for source in range(lax.axis_size(axis))]
     return lax.ppermute(value, axis, pairs)
+
+
+def after(value, *others):
+    return lax.optimization_barrier((value, *others))[0]
 
 
 def ordered(mine, other, bit):
@@ -33,7 +37,7 @@
         dq_ref, dk_acc, dv_acc, kt_ref = rest[deps:]
     else:
         far_dq_ref, dk_in, dv_in = rest[:3]
-        whole_ref, far_ref, dk_acc, dv_acc, kt_ref = rest[3 + deps :]
+        whole_ref, *far_refs, dk_acc, dv_acc, kt_ref = rest[3 + deps :]
     step = pl.program_id(0)
     steps = pl.num_programs(0)
     size = PAIR // 2
@@ -87,17 +91,20 @@
 
     @pl.when(step == steps - 1)
     def _():
-        rows = far_ref.shape[0]
+        rows = far_dq_ref.shape[0]
         dk = dk_acc[...].astype(BF16)
         dv = dv_acc[...].astype(BF16)
         whole_ref[rows:, :PAIR] = far_dq_ref[...]
         whole_ref[:, PAIR : 2 * PAIR] = dk
         whole_ref[:, 2 * PAIR :] = dv
-        far_ref[:, :PAIR] = dk[rows:]
-        far_ref[:, PAIR:] = dv[rows:]
-
-
-def attention(first, pair, slopes, qkv, grad, logd, earlier, deps):
+        size = rows // len(far_refs)
+        for number, far_ref in enumerate(far_refs):
+            cut = slice(rows + number * size, rows + (number + 1) * size)
+            far_ref[:, :PAIR] = dk[cut]
+            far_ref[:, PAIR:] = dv[cut]
+
+
+def attention(first, pair, slopes, qkv, grad, logd, earlier, deps, parts):
     both, _ = qkv.shape
     rows = both // 2
     steps = rows // TILE
@@ -111,8 +118,8 @@
         scratch = []
         earlier_specs = []
     else:
-        out_shape = (out_bf16(both, 3 * PAIR), out_bf16(rows, 2 * PAIR))
-        out_specs = (fixed(both, 3 * PAIR), fixed(rows, 2 * PAIR))
+        out_shape = (out_bf16(both, 3 * PAIR),) + (out_bf16(rows // parts, 2 * PAIR),) * parts
+        out_specs = (fixed(both, 3 * PAIR),) + (fixed(rows // parts, 2 * PAIR),) * parts
         scratch = [pltpu.VMEM((both, PAIR), F32), pltpu.VMEM((both, PAIR), F32)]
         earlier_specs = [fixed(rows, PAIR), fixed(both, PAIR), fixed(both, PAIR)]
     return pl.pallas_call(
@@ -151,7 +158,6 @@
     heads = slopes.shape[0] // 2
     pairs = width // PAIR
     half_rows = rows // 2
-    quarter = half_rows // 2
 
     def bit_of(position):
         return (me // 2**position) % 2
@@ -161,35 +167,36 @@
         pieces = (stacked[:, :, None], arrived[:, :, None])
         along = [jnp.concatenate(c, 2) for c in (pieces, pieces[::-1])]
         stacked = jnp.where(bit_of(position) == 0, along[0], along[1])
-        return stacked.reshape(2, -1, shard, 3 * width)
+        return stacked.reshape(2, -1, shard, 6 * width)
+
+    def by_side(columns):
+        return [lax.dynamic_slice_in_dim(columns, which * 3 * width, 3 * width, 1) for which in (side, 1 - side)]
+
+    with jax.named_scope("exchange_inputs"):
+        grad_mine = lax.dynamic_slice_in_dim(grad_attn, side * width, width, 1)
+        grad_theirs = lax.dynamic_slice_in_dim(grad_attn, (1 - side) * width, width, 1)
+        far_positions = flip(positions, "ctx", far_mask)
+        slopes_mine = lax.dynamic_slice_in_dim(slopes, side * heads, heads, 0)
 
     with jax.named_scope("gather_weight"):
-        weight_parts = []
-        for which in (side, 1 - side):
-            part = lax.dynamic_slice_in_dim(qkv_weight, which * width, width, 2)
-            part = part.reshape(shard, 3, pairs, PAIR).transpose(0, 2, 1, 3)
-            weight_parts.append(part.reshape(shard, 3 * width))
-        far_positions = flip(positions, "ctx", far_mask)
-        weight_far = flip(weight_parts[1], "ctx", far_mask)
-        stacked = ordered(weight_parts[0][None], weight_far[None], side)[:, None]
+        part = qkv_weight.reshape(shard, 3, 2, pairs, PAIR).transpose(0, 2, 3, 1, 4).reshape(shard, 6 * width)
+        stacked = ordered(part[None], flip(part, "ctx", far_mask)[None], side)[:, None]
         stacked, token_source = lax.optimization_barrier((stacked, tokens))
         for position in reversed(range(bits)):
             stacked = widen(stacked, position)
-        weight = stacked.reshape(model, 3 * width)
+        weight_all = stacked.reshape(model, 6 * width)
+        weight, weight_other = by_side(weight_all)
 
     with jax.named_scope("exchange_inputs"):
+        grad_far = [flip(grad_theirs[:, :PAIR], "ctx", far_mask)]
         token_half = lax.dynamic_slice_in_dim(token_source, head_side * half_rows, half_rows, 0)
+        piece = half_rows // 3
         near, cross = [], []
-        for part in range(2):
-            arrived = flip(token_half[part * quarter : (part + 1) * quarter], "ctx", far_mask)
+        for number in range(3):
+            arrived = flip(token_half[number * piece : (number + 1) * piece], "ctx", far_mask)
             near.append(arrived)
             cross.append(flip(arrived, "head", 1))
         far_tokens = ordered(jnp.concatenate(near, 0), jnp.concatenate(cross, 0), head_side)
-        grad_mine = lax.dynamic_slice_in_dim(grad_attn, side * width, width, 1)
-        grad_theirs = lax.dynamic_slice_in_dim(grad_attn, (1 - side) * width, width, 1)
-        first_theirs, _ = lax.optimization_barrier((grad_theirs[:, :PAIR], near[0]))
-        grad_far = [flip(first_theirs, "ctx", far_mask)]
-        slopes_mine = lax.dynamic_slice_in_dim(slopes, side * heads, heads, 0)
 
     with jax.named_scope("log_distance"):
         pos = jnp.concatenate([positions, far_positions], 0)
@@ -201,15 +208,15 @@
         qkv = jnp.concatenate([qkv_own, qkv_far], 0)
         both_tokens = jnp.concatenate([tokens, far_tokens], 0)
 
-    late_mine, late_theirs, *late_grads = lax.optimization_barrier(
-        (weight_parts[0], weight_parts[1], *[grad_theirs[:, p * PAIR : (p + 1) * PAIR] for p in range(1, pairs)], qkv_own)
-    )[:-1]
     with jax.named_scope("exchange_inputs"):
-        grad_far += [flip(g, "ctx", far_mask) for g in late_grads]
+        late_grad, _ = lax.optimization_barrier((grad_theirs[:, PAIR:], qkv_own))
+        grad_far += [flip(late_grad[:, p * PAIR : (p + 1) * PAIR], "ctx", far_mask) for p in range(pairs - 1)]
+
     with jax.named_scope("gather_other_weight"):
-        back = flip(late_mine, "ctx", far_mask)
-        stacked = ordered(late_theirs[None], back[None], side)[:, None]
-    positions_left = list(reversed(range(bits)))
+        core = bit_of(0)
+        core_half = lax.dynamic_slice_in_dim(weight_all, core * (model // 2), model // 2, 0)
+        core_half = after(core_half, qkv_own)
+        across_first = flip(core_half[: model // 4], "head", 1)
 
     def reduce_weight(total, position):
         bit = bit_of(position)
@@ -218,50 +225,57 @@
         keep = lax.dynamic_index_in_dim(folded, bit, 2, keepdims=False)
         return keep + flip(send, "ctx", 2**position)
 
-    deps = [stacked] + grad_far[1:]
-    wholes, others, terms = [], [], []
+    def attend(first, pair, grad, earlier, deps, parts=1):
+        with jax.named_scope("attention_far_queries" if first else "attention_own_queries"):
+            return attention(first, pair, slopes_mine, qkv, grad, logd, earlier, deps, parts)
+
+    def weight_term(whole):
+        with jax.named_scope("weight_grad"):
+            term = lax.dot_general(both_tokens, whole, (((0,), (0,)), ((), ())), preferred_element_type=F32)
+            return term.reshape(2, far_mask, shard, 3 * PAIR)
+
+    wholes, others, across_own, across_other, terms = [], [], [], [], []
+    before_far, before_own = [], grad_far[1:] + [across_first]
     for pair in range(pairs):
+        last = pair == pairs - 1
         cut = slice(pair * PAIR, (pair + 1) * PAIR)
-        with jax.named_scope("attention_far_queries"):
-            far_dq, *sums = attention(
-                True, pair, slopes_mine, qkv, grad_far[pair], logd, [], deps if pair else []
-            )
-        if pair:
-            deps = [other_rest]
+        far_dq, *sums = attend(True, pair, grad_far[pair], [], before_far)
         with jax.named_scope("return_grads"):
             other_dq = flip(far_dq, "ctx", far_mask)
-        if positions_left and pair:
+        if not pair:
             with jax.named_scope("gather_other_weight"):
-                stacked = widen(stacked, positions_left.pop(0))
+                across_second = flip(after(core_half[model // 4 :], far_dq), "head", 1)
+        if pair:
+            with jax.named_scope("return_grads"):
+                across_other[-1] = flip(after(others[-1], far_dq), "head", 1)
             with jax.named_scope("weight_grad"):
-                terms[0] = reduce_weight(terms[0], 0)
-            deps += [stacked, terms[0]]
-        with jax.named_scope("attention_own_queries"):
-            whole, far_rest = attention(
-                False, pair, slopes_mine, qkv, grad_mine[:, cut], logd, [far_dq, *sums], deps
-            )
-        deps = [other_dq]
-        if positions_left and not pair:
-            with jax.named_scope("gather_other_weight"):
-                stacked = widen(stacked, positions_left.pop(0))
-                deps.append(stacked)
+                terms[-1] = after(reduce_weight(terms[-1], 0), far_dq)
+            before_own = [others[-1], across_own[-1], terms[-1]]
+        parts = 2 if last else 1
+        whole, *far_rest = attend(False, pair, grad_mine[:, cut], [far_dq, *sums], before_own, parts)
+        before_far = [other_dq, across_second]
         with jax.named_scope("return_grads"):
-            other_rest = flip(far_rest, "ctx", far_mask)
+            if pair:
+                across_other[-1] = after(across_other[-1], whole)
+                terms[-1] = after(reduce_weight(terms[-1], 1), whole)
+            size = rows // parts
+            rest = [flip(f, "ctx", far_mask) for f in far_rest]
+            other = [jnp.concatenate([other_dq[n * size : (n + 1) * size], rest[n]], 1) for n in range(parts)]
+            others.append(other[0] if parts == 1 else jnp.concatenate(other, 0))
+            across = jnp.concatenate([flip(o, "head", 1) for o in other], 0) if last else None
+            across_own.append(flip(whole[:rows], "head", 1))
         wholes.append(whole)
-        others.append(jnp.concatenate([other_dq, other_rest], 1))
-        with jax.named_scope("weight_grad"):
-            term = lax.dot_general(both_tokens, whole, (((0,), (0,)), ((), ())), preferred_element_type=F32)
-            terms.append(term.reshape(2, far_mask, shard, 3 * PAIR))
+        across_other.append(across)
+        terms.append(weight_term(whole))
 
     with jax.named_scope("gather_other_weight"):
-        for position in positions_left:
-            stacked = widen(stacked, position)
-        weight_other = stacked.reshape(model, 3 * width)
+        across_half = jnp.concatenate([across_first, across_second], 0)
+        across_rest = flip(after(across_half, wholes[-1]), "ctx", 1)
 
     with jax.named_scope("weight_grad"):
         kept, arrived = [], []
         for pair, total in enumerate(terms):
-            for position in range(0 if pair else 1, bits):
+            for position in range(0 if pair == pairs - 1 else 2, bits):
                 total = reduce_weight(total, position)
             total = total.reshape(2, shard, 3 * PAIR)
             kept.append(lax.dynamic_index_in_dim(total, side, 0, keepdims=False))
@@ -275,22 +289,23 @@
         )
 
     with jax.named_scope("token_grad"):
-        dqkv = jnp.concatenate([w[:rows] for w in wholes] + others, 1)
-        joined = jnp.concatenate([weight, weight_other], 1)
-
-        def partial_rows(part):
-            rows_part = lax.dynamic_slice_in_dim(dqkv, part * half_rows, half_rows, 0)
-            return lax.dot_general(rows_part, joined, (((1,), (1,)), ((), ())), preferred_element_type=F32)
-
-        sent = partial_rows(1 - head_side)
-        kept = partial_rows(head_side)
-        mine, cross = [], []
-        for part in range(2):
-            cut = slice(part * quarter, (part + 1) * quarter)
-            total = (kept[cut] + flip(sent[cut], "head", 1)).astype(BF16)
-            mine.append(total)
-            cross.append(flip(total, "head", 1))
-        d_tokens = ordered(jnp.concatenate(mine, 0), jnp.concatenate(cross, 0), head_side)
+        across_all = ordered(across_half, across_rest, core)
+        across_weight, across_weight_other = by_side(across_all)
+
+        def product(pieces):
+            left = jnp.concatenate([p for p, _ in pieces], 1)
+            right = jnp.concatenate([w for _, w in pieces], 1)
+            return lax.dot_general(left, right, (((1,), (1,)), ((), ())), preferred_element_type=F32)
+
+        total = None
+        for pair in range(pairs):
+            cut = slice(pair * 3 * PAIR, (pair + 1) * 3 * PAIR)
+            early = [(wholes[pair][:rows], weight[:, cut]), (across_own[pair], across_weight[:, cut])]
+            late = [(others[pair], weight_other[:, cut]), (across_other[pair], across_weight_other[:, cut])]
+            for pieces in ([early, late] if pair == pairs - 1 else [early + late]):
+                term = product(pieces)
+                total = term if total is None else total + term
+        d_tokens = total.astype(BF16)
     return (d_tokens, d_weight)
 
 

time: 231 us -> 239 us (1.035)
  waiting for transfers between devices: 106 us -> 70.2 us
  local copies, waits for them, and re-layouts: 8.57 us -> 29.6 us
  starting transfers between devices: 32.4 us -> 43.6 us
  matrix products: 9.28 us -> 15.5 us
    ppermute x31 -> x34, waiting for transfers between devices: 106 us -> 70.2 us  [flip(): return lax.ppermute(value, axis, pairs)]
    ppermute x31 -> x34, starting transfers between devices: 32.4 us -> 43.6 us  [flip(): return lax.ppermute(value, axis, pairs)]
    reshape x6, local copies, waits for them, and re-layouts: 0.48 us -> 6.99 us  [on_device(): jnp.stack([t.reshape(shard, 3, PAIR) for t in side_terms], 2)]
    dot_general x4 -> x5, matrix products: 6.49 us -> 12.7 us  [the longest x3 9.03 us: product(): lax.dot_general(left, right, (((1,), (1,)), ((), ())), preferred_element_...]
    unnamed x24 -> x48, local copies, waits for them, and re-layouts: 1.17 us -> 6.85 us
    slice x2 -> x7, local copies, waits for them, and re-layouts: 1.96 us -> 6.01 us  [the longest x1 1.95 us: on_device(): token_half[number * piece:(number + 1) * piece]]
    concatenate x1 -> x3, local copies, waits for them, and re-layouts: 0.03 us -> 2.8 us  [the longest x1 1.01 us: ordered(): second = jnp.concatenate([other, mine], 0)]
  transfers between devices with their start and end apart: 31 -> 34, of which waited for: 14 -> 12; matrix products, arithmetic and copies ran while one was open for 13% -> 23% of each run, Pallas kernels for 25% -> 24%
where the time goes in v3:
time: 239 us; the launch traced here: 236 us
  waiting for transfers between devices  70.2 us (29%)
  Pallas kernels  57.9 us (24%)
  starting transfers between devices  43.6 us (18%)
  local copies, waits for them, and re-layouts  29.6 us (12%)
  other arithmetic  18.2 us (8%)
  matrix products  15.5 us (6%)
    ppermute x34, waiting for transfers between devices, flip(): return lax.ppermute(value, axis, pairs)  70.2 us
    pallas_call x4, Pallas kernels, attention(): pl.pallas_call(functools.partial(attention_kernel, first, len(deps)), gri...  57.9 us
    ppermute x34, starting transfers between devices, flip(): return lax.ppermute(value, axis, pairs)  43.6 us
    dot_general x3, matrix products, product(): lax.dot_general(left, right, (((1,), (1,)), ((), ())), preferred_element_...  9.03 us
    reshape x6, local copies, waits for them, and re-layouts, on_device(): jnp.stack([t.reshape(shard, 3, PAIR) for t in side_terms], 2)  6.99 us
    unnamed x48, local copies, waits for them, and re-layouts  6.85 us
    mul x1, other arithmetic, on_device(): jnp.log(jnp.abs(pos[:, None] - pos[None, :]).astype(F32) + 1.0) * LOG2E  6.08 us
  transfers between devices with their start and end apart: 34, of which 12 were waited for; matrix products, arithmetic and copies ran while one was open for 23% of the time, Pallas kernels for 24%

profile of v3, /device:TPU:0, one launch (start us, length us, event | category | flops | bytes accessed | tf_op | source)
XLA Modules:
  0.0 236.4 jit_solution(9290858880546463950)
XLA Ops:
  2.1 4.1 %collective-permute-start = (bf16[64,1536]{1,0:T(8,128)(2,1)S(1)}, bf16[64,1536]{1,0:T(8,128)(2,1)S(1)}, u32[]{:S(2)}, u32[]{:S(2)}) collective-permute-start(bf16[64,1536]{1,0:T(8,128)(2,1)S(1)} %reshape.237), channel_id=1, source_target_pairs={{0,16},{2,18},{4,20},{6,22},{8,24},{10,26},{12,28},{14,30},{16,0},... | collective-permute-start | bytes 589832 | tf_op jit(solution)/shard_map/gather_weight/ppermute | solution.py:20
  6.4 8.9 %collective-permute-done = bf16[64,1536]{1,0:T(8,128)(2,1)S(1)} collective-permute-done((bf16[64,1536]{1,0:T(8,128)(2,1)S(1)}, bf16[64,1536]{1,0:T(8,128)(2,1)S(1)}, u32[]{:S(2)}, u32[]{:S(2)}) %collective-permute-start) | collective-permute-done | bytes 196640 | tf_op jit(solution)/shard_map/gather_weight/ppermute | solution.py:20
  16.2 3.4 %collective-permute-start.10 = (s32[768]{0:T(1024)S(1)}, s32[768]{0:T(1024)S(1)}, u32[]{:S(2)}, u32[]{:S(2)}) collective-permute-start(s32[768]{0:T(1024)S(1)} %copy-done.17), channel_id=1, source_target_pairs={{0,16},{2,18},{4,20},{6,22},{8,24},{10,26},{12,28},{14,30},{16,0},... | collective-permute-start | bytes 9224 | tf_op jit(solution)/shard_map/exchange_inputs/ppermute | solution.py:20
  19.6 6.2 %collective-permute-done.1 = bf16[2,1,64,1536]{3,2,0,1:T(8,128)(2,1)S(1)} collective-permute-done((bf16[2,1,64,1536]{3,2,0,1:T(8,128)(2,1)S(1)}, bf16[2,1,64,1536]{3,2,0,1:T(8,128)(2,1)S(1)}, u32[]{:S(2)}, u32[]{:S(2)}) %collective-permute-start.1) | collective-permute-done | bytes 393248 | tf_op jit(solution)/shard_map/gather_weight/ppermute | solution.py:20
  29.3 3.3 %collective-permute-start.4 = (bf16[128,1024]{1,0:T(8,128)(2,1)S(1)}, bf16[128,1024]{1,0:T(8,128)(2,1)}, u32[]{:S(2)}, u32[]{:S(2)}) collective-permute-start(bf16[128,1024]{1,0:T(8,128)(2,1)S(1)} %get-tuple-element.56), channel_id=1, source_target_pairs={{0,16},{2,18},{4,20},{6,22},{8,24},{10,26},{12,28},{14,30},{16,0},... | collective-permute-start | bytes 786440 | tf_op jit(solution)/shard_map/exchange_inputs/ppermute | solution.py:20
  32.7 2.9 %collective-permute-start.6 = (bf16[128,1024]{1,0:T(8,128)(2,1)}, bf16[128,1024]{1,0:T(8,128)(2,1)}, u32[]{:S(2)}, u32[]{:S(2)}) collective-permute-start(bf16[128,1024]{1,0:T(8,128)(2,1)} %get-tuple-element.54), channel_id=1, source_target_pairs={{0,16},{2,18},{4,20},{6,22},{8,24},{10,26},{12,28},{14,30},{16,0},... | collective-permute-start | bytes 786440 | tf_op jit(solution)/shard_map/exchange_inputs/ppermute | solution.py:20
  36.5 24.1 %collective-permute-done.4 = bf16[128,1024]{1,0:T(8,128)(2,1)} collective-permute-done((bf16[128,1024]{1,0:T(8,128)(2,1)S(1)}, bf16[128,1024]{1,0:T(8,128)(2,1)}, u32[]{:S(2)}, u32[]{:S(2)}) %collective-permute-start.4) | collective-permute-done | bytes 262176 | tf_op jit(solution)/shard_map/exchange_inputs/ppermute | solution.py:20
  62.1 4.1 %collective-permute-done.5 = bf16[128,1024]{1,0:T(8,128)(2,1)} collective-permute-done((bf16[128,1024]{1,0:T(8,128)(2,1)}, bf16[128,1024]{1,0:T(8,128)(2,1)}, u32[]{:S(2)}, u32[]{:S(2)}) %collective-permute-start.5) | collective-permute-done | bytes 262176 | tf_op jit(solution)/shard_map/exchange_inputs/ppermute | solution.py:20
  67.7 4.1 %collective-permute-done.6 = bf16[128,1024]{1,0:T(8,128)(2,1)} collective-permute-done((bf16[128,1024]{1,0:T(8,128)(2,1)}, bf16[128,1024]{1,0:T(8,128)(2,1)}, u32[]{:S(2)}, u32[]{:S(2)}) %collective-permute-start.6) | collective-permute-done | bytes 262176 | tf_op jit(solution)/shard_map/exchange_inputs/ppermute | solution.py:20
  75.3 6.1 %log_multiply_fusion.refs_5_ = f32[1536,1536]{1,0:T(8,128)} fusion(s32[1536]{0:T(1024)S(1)} %constant_dynamic-update-slice_fusion.20), kind=kLoop, calls=%fused_computation | loop fusion | flops 11796480 | bytes 9443328 | tf_op jit(solution)/shard_map/log_distance/mul | solution.py:203
  90.6 14.9 %attention_far_queries.2 = (bf16[768,128]{1,0:T(8,128)(2,1)S(1)}, f32[1536,128]{1,0:T(8,128)S(1)}, f32[1536,128]{1,0:T(8,128)S(1)}) custom-call(f32[2]{0:T(128)S(1)} %get-tuple-element.80.refs_0_, bf16[1536,768]{1,0:T(8,128)(2,1)S(1)} %pad_maximum_fusion.1.refs_1_.refs_2_.refs_3_, bf16[1536,768]{1,0:T(8,128)(2,1)S(1)} %pad_maximum_fusion.1.refs_1_.refs_2_.refs_3_, ...), custom_call_target="tpu_custom_call" | custom-call | flops 7247757312 | bytes 37748736 | tf_op jit(solution)/shard_map/attention_far_queries/pallas_call | solution.py:125
  105.5 3.0 %collective-permute-start.15 = (bf16[768,128]{1,0:T(8,128)(2,1)S(1)}, bf16[768,128]{1,0:T(8,128)(2,1)S(1)}, u32[]{:S(2)}, u32[]{:S(2)}) collective-permute-start(bf16[768,128]{1,0:T(8,128)(2,1)S(1)} %get-tuple-element.25.refs_6_), channel_id=1, source_target_pairs={{0,16},{2,18},{4,20},{6,22},{8,24},{10,26},{12,28},{14,30},{16,0},... | collective-permute-start | bytes 589832 | tf_op jit(solution)/shard_map/return_grads/ppermute | solution.py:20
  111.8 14.5 %attention_own_queries.2 = (bf16[1536,384]{1,0:T(8,128)(2,1)S(1)}, bf16[768,256]{1,0:T(8,128)(2,1)S(1)}) custom-call(f32[2]{0:T(128)S(1)} %get-tuple-element.80.refs_0_, bf16[1536,768]{1,0:T(8,128)(2,1)} %copy-done, bf16[1536,768]{1,0:T(8,128)(2,1)} %copy-done, bf16[1536,768]{1,0:T(8,128)(2,1)} %copy-done, bf16[768,128]{1,0:T(8,128)(2,1)S(1)} %get-tuple-element.61.refs_4_, ...), custom_call_target="tpu_custom_call" | custom-call | flops 7247757312 | bytes 37748736 | tf_op jit(solution)/shard_map/attention_own_queries/pallas_call | solution.py:125
  130.8 13.9 %attention_far_queries.3 = (bf16[768,128]{1,0:T(8,128)(2,1)S(1)}, f32[1536,128]{1,0:T(8,128)S(1)}, f32[1536,128]{1,0:T(8,128)S(1)}) custom-call(f32[2]{0:T(128)S(1)} %get-tuple-element.79.refs_0_, bf16[1536,768]{1,0:T(8,128)(2,1)S(1)} %copy-done.1, bf16[1536,768]{1,0:T(8,128)(2,1)S(1)} %copy-done.1, bf16[1536,768]{1,0:T(8,128)(2,1)S(1)} %copy-done.1, ...), custom_call_target="tpu_custom_call" | custom-call | flops 7247757312 | bytes 37748736 | tf_op jit(solution)/shard_map/attention_far_queries/pallas_call | solution.py:125
  150.1 14.6 %attention_own_queries.3 = (bf16[1536,384]{1,0:T(8,128)(2,1)S(1)}, bf16[384,256]{1,0:T(8,128)(2,1)S(1)}, bf16[384,256]{1,0:T(8,128)(2,1)S(1)}) custom-call(f32[2]{0:T(128)S(1)} %get-tuple-element.79.refs_0_, bf16[1536,768]{1,0:T(8,128)(2,1)} %copy-done, bf16[1536,768]{1,0:T(8,128)(2,1)} %copy-done, bf16[1536,768]{1,0:T(8,128)(2,1)} %copy-done, ...), custom_call_target="tpu_custom_call" | custom-call | flops 7247757312 | bytes 37748736 | tf_op jit(solution)/shard_map/attention_own_queries/pallas_call | solution.py:125
  170.7 7.5 %collective-permute-done.27 = f32[2,2,64,384]{3,2,1,0:T(8,128)S(1)} collective-permute-done((f32[2,2,64,384]{3,2,1,0:T(8,128)S(1)}, f32[2,2,64,384]{3,2,1,0:T(8,128)S(1)}, u32[]{:S(2)}, u32[]{:S(2)}) %collective-permute-start.27) | collective-permute-done | bytes 393248 | tf_op jit(solution)/shard_map/return_grads/ppermute | solution.py:20
  178.6 2.1 collective-permute-start.28
  180.8 5.9 %collective-permute-done.24 = bf16[384,256]{1,0:T(8,128)(2,1)S(1)} collective-permute-done((bf16[384,256]{1,0:T(8,128)(2,1)S(1)}, bf16[384,256]{1,0:T(8,128)(2,1)S(1)}, u32[]{:S(2)}, u32[]{:S(2)}) %collective-permute-start.24) | collective-permute-done | bytes 196640 | tf_op jit(solution)/shard_map/return_grads/ppermute | solution.py:20
  193.5 3.5 %collective-permute-done.30 = f32[2,2,64,384]{3,2,1,0:T(8,128)S(1)} collective-permute-done((f32[2,2,64,384]{3,2,1,0:T(8,128)S(1)}, f32[2,2,64,384]{3,2,1,0:T(8,128)S(1)}, u32[]{:S(2)}, u32[]{:S(2)}) %collective-permute-start.30) | collective-permute-done | bytes 393248 | tf_op jit(solution)/shard_map/weight_grad/ppermute | solution.py:20
  198.3 3.0 %collective-permute-start.32 = (f32[64,384]{1,0:T(8,128)}, f32[64,384]{1,0:T(8,128)}, u32[]{:S(2)}, u32[]{:S(2)}) collective-permute-start(f32[64,384]{1,0:T(8,128)} %get-tuple-element.72), channel_id=1, source_target_pairs={{0,16},{2,18},{4,20},{6,22},{8,24},{10,26},{12,28},{14,30},{16,0},... | collective-permute-start | bytes 294920 | tf_op jit(solution)/shard_map/weight_grad/ppermute | solution.py:20
  222.2 2.6 %maximum_select_fusion.1 = bf16[1024,1536]{1,0:T(8,128)(2,1)S(1)} fusion(bf16[512,1536]{1,0:T(8,128)(2,1)} %collective-permute-done.20, bf16[256,1536]{1,0:T(8,128)(2,1)S(1)} %collective-permute-done.17.refs_7_, bf16[256,1536]{1,0:T(8,128)(2,1)S(1)} %collective-permute-done.13.refs_10_, pred[]{:T(512)S(6)} %eq.28), kind=kLoop, calls=%fused_computation.3 | loop fusion | flops 20447232 | bytes 6291457 | tf_op jit(solution)/shard_map/token_grad/jit(_where)/select_n | solution.py:30
  227.0 2.6 %fusion = f32[768,1024]{1,0:T(8,128)S(1)} fusion(bf16[768,1536]{1,0:T(8,128)(2,1)S(1)} %copy-done.16, bf16[1024,384]{1,0:T(8,128)(2,1)S(1)} %get-tuple-element.49, bf16[1024,384]{1,0:T(8,128)(2,1)S(1)} %copy-done.5, bf16[1024,384]{1,0:T(8,128)(2,1)S(1)} %get-tuple-element.50, bf16[1024,384]{1,0:T(8,128)(2,1)S(1)} %copy-done.6), kind=kOutput, calls=%fused_computation.4 | convolution fusion | flops 2428502016 | bytes 8650752 | tf_op jit(solution)/shard_map/token_grad/dot_general | solution.py:298
  229.7 2.8 %fusion.10 = f32[768,1024]{1,0:T(8,128)S(1)} fusion(bf16[1024,384]{1,0:T(8,128)(2,1)S(1)} %get-tuple-element.51, bf16[1024,384]{1,0:T(8,128)(2,1)S(1)} %copy-done.4, bf16[768,384]{1,0:T(8,128)(2,1)} %collective-permute-done.21, bf16[768,384]{1,0:T(8,128)(2,1)} %slice.89), kind=kOutput, calls=%fused_computation.18 | convolution fusion | flops 1213464576 | bytes 5898240 | tf_op jit(solution)/shard_map/token_grad/dot_general | solution.py:298
  232.5 3.7 %add_convert_fusion = bf16[768,1024]{1,0:T(8,128)(2,1)} fusion(f32[768,1024]{1,0:T(8,128)S(1)} %fusion, f32[768,1024]{1,0:T(8,128)S(1)} %fusion.10, bf16[1024,384]{1,0:T(8,128)(2,1)S(1)} %get-tuple-element.48, bf16[1024,384]{1,0:T(8,128)(2,1)S(1)} %copy-done.3, bf16[384,384]{1,0:T(8,128)(2,1)} %collective-permute-done.26, ...), kind=kOutput, calls=%fused_computation.12 | convolution fusion | flops 1220542464 | bytes 10616832 | tf_op jit(solution)/shard_map/token_grad/dot_general | solution.py:298
  (163 shorter events, 73.1 us)
Async XLA Ops:
  2.1 13.2 %collective-permute-start = (bf16[64,1536]{1,0:T(8,128)(2,1)S(1)}, bf16[64,1536]{1,0:T(8,128)(2,1)S(1)}, u32[]{:S(2)}, u32[]{:S(2)}) collective-permute-start(bf16[64,1536]{1,0:T(8,128)(2,1)S(1)} %reshape.237), channel_id=1, source_target_pairs={{0,16},{2,18},{4,20},{6,22},{8,24},{10,26},{12,28},{14,30},{16,0},... | collective-permute-start | bytes 589832 | tf_op jit(solution)/shard_map/gather_weight/ppermute | solution.py:20
  16.2 20.2 %collective-permute-start.10 = (s32[768]{0:T(1024)S(1)}, s32[768]{0:T(1024)S(1)}, u32[]{:S(2)}, u32[]{:S(2)}) collective-permute-start(s32[768]{0:T(1024)S(1)} %copy-done.17), channel_id=1, source_target_pairs={{0,16},{2,18},{4,20},{6,22},{8,24},{10,26},{12,28},{14,30},{16,0},... | collective-permute-start | bytes 9224 | tf_op jit(solution)/shard_map/exchange_inputs/ppermute | solution.py:20
  26.0 47.4 %collective-permute-start.2 = (bf16[2,2,64,1536]{3,2,1,0:T(8,128)(2,1)S(1)}, bf16[2,2,64,1536]{3,2,1,0:T(8,128)(2,1)}, u32[]{:S(2)}, u32[]{:S(2)}) collective-permute-start(bf16[2,2,64,1536]{3,2,1,0:T(8,128)(2,1)S(1)} %maximum_select_fusion.4), channel_id=1, source_target_pairs={{0,4},{2,6},{4,0},{6,2},{8,12},{10,14},{12,8},{14,10},{16,20},{18,... | collective-permute-start | bytes 2359304 | tf_op jit(solution)/shard_map/gather_weight/ppermute | solution.py:20
  29.3 31.2 %collective-permute-start.4 = (bf16[128,1024]{1,0:T(8,128)(2,1)S(1)}, bf16[128,1024]{1,0:T(8,128)(2,1)}, u32[]{:S(2)}, u32[]{:S(2)}) collective-permute-start(bf16[128,1024]{1,0:T(8,128)(2,1)S(1)} %get-tuple-element.56), channel_id=1, source_target_pairs={{0,16},{2,18},{4,20},{6,22},{8,24},{10,26},{12,28},{14,30},{16,0},... | collective-permute-start | bytes 786440 | tf_op jit(solution)/shard_map/exchange_inputs/ppermute | solution.py:20
  32.6 33.5 %collective-permute-start.5 = (bf16[128,1024]{1,0:T(8,128)(2,1)}, bf16[128,1024]{1,0:T(8,128)(2,1)}, u32[]{:S(2)}, u32[]{:S(2)}) collective-permute-start(bf16[128,1024]{1,0:T(8,128)(2,1)} %get-tuple-element.55), channel_id=1, source_target_pairs={{0,16},{2,18},{4,20},{6,22},{8,24},{10,26},{12,28},{14,30},{16,0},... | collective-permute-start | bytes 786440 | tf_op jit(solution)/shard_map/exchange_inputs/ppermute | solution.py:20
  32.7 39.1 %collective-permute-start.6 = (bf16[128,1024]{1,0:T(8,128)(2,1)}, bf16[128,1024]{1,0:T(8,128)(2,1)}, u32[]{:S(2)}, u32[]{:S(2)}) collective-permute-start(bf16[128,1024]{1,0:T(8,128)(2,1)} %get-tuple-element.54), channel_id=1, source_target_pairs={{0,16},{2,18},{4,20},{6,22},{8,24},{10,26},{12,28},{14,30},{16,0},... | collective-permute-start | bytes 786440 | tf_op jit(solution)/shard_map/exchange_inputs/ppermute | solution.py:20
  36.4 54.2 %collective-permute-start.11 = (bf16[768,128]{1,0:T(8,128)(2,1)S(1)}, bf16[768,128]{1,0:T(8,128)(2,1)S(1)}, u32[]{:S(2)}, u32[]{:S(2)}) collective-permute-start(bf16[768,128]{1,0:T(8,128)(2,1)S(1)} %get-tuple-element.60), channel_id=1, source_target_pairs={{0,16},{2,18},{4,20},{6,22},{8,24},{10,26},{12,28},{14,30},{16,0},... | collective-permute-start | bytes 589832 | tf_op jit(solution)/shard_map/exchange_inputs/ppermute | solution.py:20
  60.6 20.8 %collective-permute-start.7 = (bf16[128,1024]{1,0:T(8,128)(2,1)}, bf16[128,1024]{1,0:T(8,128)(2,1)S(1)}, u32[]{:S(2)}, u32[]{:S(2)}) collective-permute-start(bf16[128,1024]{1,0:T(8,128)(2,1)} %collective-permute-done.4), channel_id=1, source_target_pairs={{0,1},{1,0},{2,3},{3,2},{4,5},{5,4},{6,7},{7,6},{8,9},{9,8},{10,11... | collective-permute-start | bytes 786440 | tf_op jit(solution)/shard_map/exchange_inputs/ppermute | solution.py:20
  66.2 15.2 %collective-permute-start.8 = (bf16[128,1024]{1,0:T(8,128)(2,1)}, bf16[128,1024]{1,0:T(8,128)(2,1)S(1)}, u32[]{:S(2)}, u32[]{:S(2)}) collective-permute-start(bf16[128,1024]{1,0:T(8,128)(2,1)} %collective-permute-done.5), channel_id=1, source_target_pairs={{0,1},{1,0},{2,3},{3,2},{4,5},{5,4},{6,7},{7,6},{8,9},{9,8},{10,11... | collective-permute-start | bytes 786440 | tf_op jit(solution)/shard_map/exchange_inputs/ppermute | solution.py:20
  89.6 22.2 %collective-permute-start.12 = (bf16[768,128]{1,0:T(8,128)(2,1)}, bf16[768,128]{1,0:T(8,128)(2,1)S(1)}, u32[]{:S(2)}, u32[]{:S(2)}) collective-permute-start(bf16[768,128]{1,0:T(8,128)(2,1)} %get-tuple-element.28), channel_id=1, source_target_pairs={{0,16},{2,18},{4,20},{6,22},{8,24},{10,26},{12,28},{14,30},{16,0},... | collective-permute-start | bytes 589832 | tf_op jit(solution)/shard_map/exchange_inputs/ppermute | solution.py:20
  89.9 21.9 %collective-permute-start.13 = (bf16[256,1536]{1,0:T(8,128)(2,1)S(1)}, bf16[256,1536]{1,0:T(8,128)(2,1)S(1)}, u32[]{:S(2)}, u32[]{:S(2)}) collective-permute-start(bf16[256,1536]{1,0:T(8,128)(2,1)S(1)} %get-tuple-element.53), channel_id=1, source_target_pairs={{0,1},{1,0},{2,3},{3,2},{4,5},{5,4},{6,7},{7,6},{8,9},{9,8},{10,11... | collective-permute-start | bytes 2359304 | tf_op jit(solution)/shard_map/gather_other_weight/ppermute | solution.py:20
  105.5 25.3 %collective-permute-start.15 = (bf16[768,128]{1,0:T(8,128)(2,1)S(1)}, bf16[768,128]{1,0:T(8,128)(2,1)S(1)}, u32[]{:S(2)}, u32[]{:S(2)}) collective-permute-start(bf16[768,128]{1,0:T(8,128)(2,1)S(1)} %get-tuple-element.25.refs_6_), channel_id=1, source_target_pairs={{0,16},{2,18},{4,20},{6,22},{8,24},{10,26},{12,28},{14,30},{16,0},... | collective-permute-start | bytes 589832 | tf_op jit(solution)/shard_map/return_grads/ppermute | solution.py:20
  108.5 22.3 %collective-permute-start.17 = (bf16[256,1536]{1,0:T(8,128)(2,1)S(1)}, bf16[256,1536]{1,0:T(8,128)(2,1)S(1)}, u32[]{:S(2)}, u32[]{:S(2)}) collective-permute-start(bf16[256,1536]{1,0:T(8,128)(2,1)S(1)} %get-tuple-element.32), channel_id=1, source_target_pairs={{0,1},{1,0},{2,3},{3,2},{4,5},{5,4},{6,7},{7,6},{8,9},{9,8},{10,11... | collective-permute-start | bytes 2359304 | tf_op jit(solution)/shard_map/gather_other_weight/ppermute | solution.py:20
  129.1 17.6 %collective-permute-start.14 = (bf16[768,384]{1,0:T(8,128)(2,1)S(1)}, bf16[768,384]{1,0:T(8,128)(2,1)S(1)}, u32[]{:S(2)}, u32[]{:S(2)}) collective-permute-start(bf16[768,384]{1,0:T(8,128)(2,1)S(1)} %get-tuple-element.57), channel_id=1, source_target_pairs={{0,1},{1,0},{2,3},{3,2},{4,5},{5,4},{6,7},{7,6},{8,9},{9,8},{10,11... | collective-permute-start | bytes 1769480 | tf_op jit(solution)/shard_map/return_grads/ppermute | solution.py:20
  129.6 19.6 %collective-permute-start.16 = (bf16[768,256]{1,0:T(8,128)(2,1)S(1)}, bf16[768,256]{1,0:T(8,128)(2,1)S(1)}, u32[]{:S(2)}, u32[]{:S(2)}) collective-permute-start(bf16[768,256]{1,0:T(8,128)(2,1)S(1)} %get-tuple-element.31), channel_id=1, source_target_pairs={{0,16},{2,18},{4,20},{6,22},{8,24},{10,26},{12,28},{14,30},{16,0},... | collective-permute-start | bytes 1179656 | tf_op jit(solution)/shard_map/return_grads/ppermute | solution.py:20
  130.7 19.3 %collective-permute-start.19 = (f32[2,4,64,384]{3,2,1,0:T(8,128)S(1)}, f32[2,4,64,384]{3,2,1,0:T(8,128)S(1)}, u32[]{:S(2)}, u32[]{:S(2)}) collective-permute-start(f32[2,4,64,384]{3,2,1,0:T(8,128)S(1)} %dynamic-slice_bitcast_fusion.1), channel_id=1, source_target_pairs={{0,2},{2,0},{4,6},{6,4},{8,10},{10,8},{12,14},{14,12},{16,18},{18,... | collective-permute-start | bytes 2359304 | tf_op jit(solution)/shard_map/weight_grad/ppermute | solution.py:20
  144.7 22.7 %collective-permute-start.22 = (bf16[768,128]{1,0:T(8,128)(2,1)S(1)}, bf16[768,128]{1,0:T(8,128)(2,1)S(1)}, u32[]{:S(2)}, u32[]{:S(2)}) collective-permute-start(bf16[768,128]{1,0:T(8,128)(2,1)S(1)} %get-tuple-element.33.refs_6_), channel_id=1, source_target_pairs={{0,16},{2,18},{4,20},{6,22},{8,24},{10,26},{12,28},{14,30},{16,0},... | collective-permute-start | bytes 589832 | tf_op jit(solution)/shard_map/return_grads/ppermute | solution.py:20
  167.5 24.6 %collective-permute-start.18 = (bf16[768,384]{1,0:T(8,128)(2,1)S(1)}, bf16[768,384]{1,0:T(8,128)(2,1)S(1)}, u32[]{:S(2)}, u32[]{:S(2)}) collective-permute-start(bf16[768,384]{1,0:T(8,128)(2,1)S(1)} %get-tuple-element.34.refs_9_), channel_id=1, source_target_pairs={{0,1},{1,0},{2,3},{3,2},{4,5},{5,4},{6,7},{7,6},{8,9},{9,8},{10,11... | collective-permute-start | bytes 1769480 | tf_op jit(solution)/shard_map/return_grads/ppermute | solution.py:20
  169.8 52.4 %collective-permute-start.20 = (bf16[512,1536]{1,0:T(8,128)(2,1)S(1)}, bf16[512,1536]{1,0:T(8,128)(2,1)}, u32[]{:S(2)}, u32[]{:S(2)}) collective-permute-start(bf16[512,1536]{1,0:T(8,128)(2,1)S(1)} %pad_maximum_fusion.4), channel_id=1, source_target_pairs={{0,2},{2,0},{4,6},{6,4},{8,10},{10,8},{12,14},{14,12},{16,18},{18,... | collective-permute-start | bytes 4718600 | tf_op jit(solution)/shard_map/gather_other_weight/ppermute | solution.py:20
  169.8 17.0 %collective-permute-start.24 = (bf16[384,256]{1,0:T(8,128)(2,1)S(1)}, bf16[384,256]{1,0:T(8,128)(2,1)S(1)}, u32[]{:S(2)}, u32[]{:S(2)}) collective-permute-start(bf16[384,256]{1,0:T(8,128)(2,1)S(1)} %get-tuple-element.42), channel_id=1, source_target_pairs={{0,16},{2,18},{4,20},{6,22},{8,24},{10,26},{12,28},{14,30},{16,0},... | collective-permute-start | bytes 589832 | tf_op jit(solution)/shard_map/return_grads/ppermute | solution.py:20
  178.6 14.8 %collective-permute-start.28 = (f32[2,1,64,384]{3,2,1,0:T(8,128)S(1)}, f32[2,1,64,384]{3,2,1,0:T(8,128)S(1)}, u32[]{:S(2)}, u32[]{:S(2)}) collective-permute-start(f32[2,1,64,384]{3,2,1,0:T(8,128)S(1)} %constant_dynamic-slice_fusion.12), channel_id=1, source_target_pairs={{0,8},{2,10},{4,12},{6,14},{8,0},{10,2},{12,4},{14,6},{16,24},{18,... | collective-permute-start | bytes 589832 | tf_op jit(solution)/shard_map/weight_grad/ppermute | solution.py:20
  190.6 39.0 %collective-permute-start.21 = (bf16[768,384]{1,0:T(8,128)(2,1)}, bf16[768,384]{1,0:T(8,128)(2,1)}, u32[]{:S(2)}, u32[]{:S(2)}) collective-permute-start(bf16[768,384]{1,0:T(8,128)(2,1)} %slice.89), channel_id=1, source_target_pairs={{0,1},{1,0},{2,3},{3,2},{4,5},{5,4},{6,7},{7,6},{8,9},{9,8},{10,11... | collective-permute-start | bytes 1769480 | tf_op jit(solution)/shard_map/return_grads/ppermute | solution.py:20
  192.1 40.4 %collective-permute-start.26 = (bf16[384,384]{1,0:T(8,128)(2,1)}, bf16[384,384]{1,0:T(8,128)(2,1)}, u32[]{:S(2)}, u32[]{:S(2)}) collective-permute-start(bf16[384,384]{1,0:T(8,128)(2,1)} %pad_maximum_fusion.7), channel_id=1, source_target_pairs={{0,1},{1,0},{2,3},{3,2},{4,5},{5,4},{6,7},{7,6},{8,9},{9,8},{10,11... | collective-permute-start | bytes 884744 | tf_op jit(solution)/shard_map/return_grads/ppermute | solution.py:20
  205.4 27.1 %collective-permute-start.25 = (bf16[384,384]{1,0:T(8,128)(2,1)}, bf16[384,384]{1,0:T(8,128)(2,1)}, u32[]{:S(2)}, u32[]{:S(2)}) collective-permute-start(bf16[384,384]{1,0:T(8,128)(2,1)} %pad_maximum_fusion.6), channel_id=1, source_target_pairs={{0,1},{1,0},{2,3},{3,2},{4,5},{5,4},{6,7},{7,6},{8,9},{9,8},{10,11... | collective-permute-start | bytes 884744 | tf_op jit(solution)/shard_map/return_grads/ppermute | solution.py:20
  (29 other events, 267.2 us)

commit v4 on v3

--- a/solution.py
+++ b/solution.py
@@ -30,14 +30,15 @@
     return jnp.where(bit == 0, first, second)
 
 
-def attention_kernel(first, deps, *refs):
+def attention_kernel(last, start, held, done, deps, *refs):
     slope_ref, q_ref, k_ref, v_ref, g_ref, logd_ref = refs[:6]
     rest = refs[6:]
-    if first:
-        dq_ref, dk_acc, dv_acc, kt_ref = rest[deps:]
+    sums_in, rest = rest[:held], rest[held:]
+    dq_in, rest = rest[:done], rest[done + deps :]
+    if last:
+        whole_ref, *far_refs, dk_acc, dv_acc, kt_ref = rest
     else:
-        far_dq_ref, dk_in, dv_in = rest[:3]
-        whole_ref, *far_refs, dk_acc, dv_acc, kt_ref = rest[3 + deps :]
+        dq_ref, dk_acc, dv_acc, kt_ref = rest
     step = pl.program_id(0)
     steps = pl.num_programs(0)
     size = PAIR // 2
@@ -46,12 +47,12 @@
     @pl.when(step == 0)
     def _():
         kt_ref[...] = k_ref[...].astype(F32).T.astype(BF16)
-        if first:
+        if held:
+            dk_acc[...] = sums_in[0][...]
+            dv_acc[...] = sums_in[1][...]
+        else:
             dk_acc[...] = jnp.zeros_like(dk_acc)
             dv_acc[...] = jnp.zeros_like(dv_acc)
-        else:
-            dk_acc[...] = dk_in[...]
-            dv_acc[...] = dv_in[...]
 
     lane = lax.broadcasted_iota(jnp.int32, (TILE, PAIR), 1)
     key = k_ref[...]
@@ -83,18 +84,20 @@
         grads_q.append(grad_q[head * size : (head + 1) * size])
     grad_q = jnp.concatenate(grads_q, 0).T.astype(BF16)
 
-    if first:
+    if not last:
         dq_ref[...] = grad_q
         return
 
-    whole_ref[pl.ds(pl.multiple_of(step * TILE, TILE), TILE), :PAIR] = grad_q
+    whole_ref[pl.ds(pl.multiple_of((start + step) * TILE, TILE), TILE), :PAIR] = grad_q
 
     @pl.when(step == steps - 1)
     def _():
-        rows = far_dq_ref.shape[0]
+        rows = whole_ref.shape[0] // 2
         dk = dk_acc[...].astype(BF16)
         dv = dv_acc[...].astype(BF16)
-        whole_ref[rows:, :PAIR] = far_dq_ref[...]
+        whole_ref[rows:, :PAIR] = dq_in[0][...]
+        if done > 1:
+            whole_ref[: start * TILE, :PAIR] = dq_in[1][...]
         whole_ref[:, PAIR : 2 * PAIR] = dk
         whole_ref[:, 2 * PAIR :] = dv
         size = rows // len(far_refs)
@@ -104,26 +107,23 @@
             far_ref[:, PAIR:] = dv[cut]
 
 
-def attention(first, pair, slopes, qkv, grad, logd, earlier, deps, parts):
+def attention(pair, start, stop, slopes, qkv, grad, logd, sums, dqs, deps, parts):
     both, _ = qkv.shape
     rows = both // 2
-    steps = rows // TILE
-    start = steps if first else 0
+    steps = stop - start
     acc = jax.ShapeDtypeStruct((both, PAIR), F32)
     fixed = lambda *shape: pl.BlockSpec(shape, lambda i: (0, 0))
     out_bf16 = lambda *shape: jax.ShapeDtypeStruct(shape, BF16)
-    if first:
-        out_shape = (out_bf16(rows, PAIR), acc, acc)
-        out_specs = (pl.BlockSpec((TILE, PAIR), lambda i: (i, 0)), fixed(both, PAIR), fixed(both, PAIR))
-        scratch = []
-        earlier_specs = []
-    else:
+    if parts:
         out_shape = (out_bf16(both, 3 * PAIR),) + (out_bf16(rows // parts, 2 * PAIR),) * parts
         out_specs = (fixed(both, 3 * PAIR),) + (fixed(rows // parts, 2 * PAIR),) * parts
         scratch = [pltpu.VMEM((both, PAIR), F32), pltpu.VMEM((both, PAIR), F32)]
-        earlier_specs = [fixed(rows, PAIR), fixed(both, PAIR), fixed(both, PAIR)]
+    else:
+        out_shape = (out_bf16(steps * TILE, PAIR), acc, acc)
+        out_specs = (pl.BlockSpec((TILE, PAIR), lambda i: (i, 0)), fixed(both, PAIR), fixed(both, PAIR))
+        scratch = []
     return pl.pallas_call(
-        functools.partial(attention_kernel, first, len(deps)),
+        functools.partial(attention_kernel, bool(parts), start, len(sums), len(dqs), len(deps)),
         grid=(steps,),
         out_shape=out_shape,
         in_specs=[
@@ -134,7 +134,8 @@
             pl.BlockSpec((TILE, PAIR), lambda i: (i, 0)),
             pl.BlockSpec((both, TILE), lambda i: (0, start + i)),
         ]
-        + earlier_specs
+        + [fixed(both, PAIR)] * len(sums)
+        + [fixed(*dq.shape) for dq in dqs]
         + [pl.BlockSpec(memory_space=pl.ANY)] * len(deps),
         out_specs=out_specs,
         scratch_shapes=scratch + [pltpu.VMEM((PAIR, both), BF16)],
@@ -142,7 +143,29 @@
         cost_estimate=pl.CostEstimate(
             flops=24 * both * both * PAIR, bytes_accessed=16 * both * both, transcendentals=2 * both * both
         ),
-    )(slopes[2 * pair : 2 * pair + 2], qkv, qkv, qkv, grad, logd, *earlier, *deps)
+    )(slopes[2 * pair : 2 * pair + 2], qkv, qkv, qkv, grad, logd, *sums, *dqs, *deps)
+
+
+def assemble_kernel(side_ref, kept_ref, arrived_ref, _, out_ref):
+    pairs = kept_ref.shape[1] // (3 * PAIR)
+    for which in range(2):
+        here = side_ref[0] == which
+        for pair in range(pairs):
+            for third in range(3):
+                source = pl.ds((pair * 3 + third) * PAIR, PAIR)
+                value = jnp.where(here, kept_ref[:, source], arrived_ref[:, source])
+                out_ref[:, third, pl.ds((which * pairs + pair) * PAIR, PAIR)] = value
+
+
+def assemble(side, kept, arrived, earlier):
+    shard, columns = kept.shape
+    vmem = pl.BlockSpec(memory_space=pltpu.VMEM)
+    return pl.pallas_call(
+        assemble_kernel,
+        out_shape=jax.ShapeDtypeStruct((shard, 3, 2 * columns // 3), F32),
+        in_specs=[pl.BlockSpec(memory_space=pltpu.SMEM), vmem, vmem, pl.BlockSpec(memory_space=pl.ANY)],
+        out_specs=vmem,
+    )(side.astype(jnp.int32).reshape(1), kept, arrived, earlier)
 
 
 def on_device(tokens, qkv_weight, grad_attn, positions, slopes):
@@ -181,21 +204,23 @@
     with jax.named_scope("gather_weight"):
         part = qkv_weight.reshape(shard, 3, 2, pairs, PAIR).transpose(0, 2, 3, 1, 4).reshape(shard, 6 * width)
         stacked = ordered(part[None], flip(part, "ctx", far_mask)[None], side)[:, None]
-        stacked, token_source = lax.optimization_barrier((stacked, tokens))
         for position in reversed(range(bits)):
             stacked = widen(stacked, position)
         weight_all = stacked.reshape(model, 6 * width)
         weight, weight_other = by_side(weight_all)
 
     with jax.named_scope("exchange_inputs"):
-        grad_far = [flip(grad_theirs[:, :PAIR], "ctx", far_mask)]
-        token_half = lax.dynamic_slice_in_dim(token_source, head_side * half_rows, half_rows, 0)
+        token_half = lax.dynamic_slice_in_dim(tokens, head_side * half_rows, half_rows, 0)
         piece = half_rows // 3
         near, cross = [], []
         for number in range(3):
-            arrived = flip(token_half[number * piece : (number + 1) * piece], "ctx", far_mask)
+            source = token_half[number * piece : (number + 1) * piece]
+            if number:
+                source = after(source, near[-1])
+            arrived = flip(source, "ctx", far_mask)
             near.append(arrived)
             cross.append(flip(arrived, "head", 1))
+        grad_far = [flip(after(grad_theirs[:, :PAIR], near[1]), "ctx", far_mask)]
         far_tokens = ordered(jnp.concatenate(near, 0), jnp.concatenate(cross, 0), head_side)
 
     with jax.named_scope("log_distance"):
@@ -218,28 +243,18 @@
         core_half = after(core_half, qkv_own)
         across_first = flip(core_half[: model // 4], "head", 1)
 
-    def reduce_weight(total, position):
-        bit = bit_of(position)
-        folded = total.reshape(2, total.shape[1] // 2, 2, shard, total.shape[-1])
-        send = lax.dynamic_index_in_dim(folded, 1 - bit, 2, keepdims=False)
-        keep = lax.dynamic_index_in_dim(folded, bit, 2, keepdims=False)
-        return keep + flip(send, "ctx", 2**position)
-
-    def attend(first, pair, grad, earlier, deps, parts=1):
-        with jax.named_scope("attention_far_queries" if first else "attention_own_queries"):
-            return attention(first, pair, slopes_mine, qkv, grad, logd, earlier, deps, parts)
-
-    def weight_term(whole):
-        with jax.named_scope("weight_grad"):
-            term = lax.dot_general(both_tokens, whole, (((0,), (0,)), ((), ())), preferred_element_type=F32)
-            return term.reshape(2, far_mask, shard, 3 * PAIR)
-
-    wholes, others, across_own, across_other, terms = [], [], [], [], []
+    tiles = rows // TILE
+
+    def attend(pair, start, stop, grad, sums, dqs, deps, parts=0):
+        with jax.named_scope("attention"):
+            return attention(pair, start, stop, slopes_mine, qkv, grad, logd, sums, dqs, deps, parts)
+
+    wholes, others, across_own, across_other = [], [], [], []
     before_far, before_own = [], grad_far[1:] + [across_first]
     for pair in range(pairs):
         last = pair == pairs - 1
         cut = slice(pair * PAIR, (pair + 1) * PAIR)
-        far_dq, *sums = attend(True, pair, grad_far[pair], [], before_far)
+        far_dq, *sums = attend(pair, tiles, 2 * tiles, grad_far[pair], [], [], before_far)
         with jax.named_scope("return_grads"):
             other_dq = flip(far_dq, "ctx", far_mask)
         if not pair:
@@ -248,45 +263,49 @@
         if pair:
             with jax.named_scope("return_grads"):
                 across_other[-1] = flip(after(others[-1], far_dq), "head", 1)
-            with jax.named_scope("weight_grad"):
-                terms[-1] = after(reduce_weight(terms[-1], 0), far_dq)
-            before_own = [others[-1], across_own[-1], terms[-1]]
+            before_own = [others[-1], across_own[-1], across_second]
         parts = 2 if last else 1
-        whole, *far_rest = attend(False, pair, grad_mine[:, cut], [far_dq, *sums], before_own, parts)
-        before_far = [other_dq, across_second]
+        dqs, begin = [far_dq], 0
+        if last:
+            begin = tiles - 1
+            own_dq, *sums = attend(pair, 0, begin, grad_mine[: begin * TILE, cut], sums, [], before_own)
+            dqs.append(own_dq)
+            before_own = [across_other[-1], other_dq]
+        whole, *far_rest = attend(pair, begin, tiles, grad_mine[begin * TILE :, cut], sums, dqs, before_own, parts)
+        before_far = [other_dq]
         with jax.named_scope("return_grads"):
-            if pair:
-                across_other[-1] = after(across_other[-1], whole)
-                terms[-1] = after(reduce_weight(terms[-1], 1), whole)
             size = rows // parts
             rest = [flip(f, "ctx", far_mask) for f in far_rest]
-            other = [jnp.concatenate([other_dq[n * size : (n + 1) * size], rest[n]], 1) for n in range(parts)]
-            others.append(other[0] if parts == 1 else jnp.concatenate(other, 0))
-            across = jnp.concatenate([flip(o, "head", 1) for o in other], 0) if last else None
+            others.append(None if last else jnp.concatenate([other_dq, rest[0]], 1))
             across_own.append(flip(whole[:rows], "head", 1))
         wholes.append(whole)
-        across_other.append(across)
-        terms.append(weight_term(whole))
+        across_other.append(None)
 
     with jax.named_scope("gather_other_weight"):
         across_half = jnp.concatenate([across_first, across_second], 0)
         across_rest = flip(after(across_half, wholes[-1]), "ctx", 1)
 
     with jax.named_scope("weight_grad"):
-        kept, arrived = [], []
-        for pair, total in enumerate(terms):
-            for position in range(0 if pair == pairs - 1 else 2, bits):
-                total = reduce_weight(total, position)
-            total = total.reshape(2, shard, 3 * PAIR)
-            kept.append(lax.dynamic_index_in_dim(total, side, 0, keepdims=False))
-            arrived.append(flip(lax.dynamic_index_in_dim(total, 1 - side, 0, keepdims=False), "ctx", far_mask))
-        kept, arrived = [
-            jnp.stack([t.reshape(shard, 3, PAIR) for t in side_terms], 2).reshape(shard, 3, width)
-            for side_terms in (kept, arrived)
+        total = lax.dot_general(
+            both_tokens, jnp.concatenate(wholes, 1), (((0,), (0,)), ((), ())), preferred_element_type=F32
+        ).reshape(2, far_mask // 2, 2, shard, 3 * width)
+        total = lax.dynamic_index_in_dim(total, core, 2, keepdims=False) + flip(
+            lax.dynamic_index_in_dim(total, 1 - core, 2, keepdims=False), "ctx", 1
+        )
+        group = (me % far_mask) // 2
+        pieces = [lax.dynamic_index_in_dim(total, group, 1, keepdims=False)]
+        sends = [
+            lax.dynamic_index_in_dim(total, jnp.bitwise_xor(group, apart), 1, keepdims=False)
+            for apart in range(1, far_mask // 2)
         ]
-        d_weight = jnp.where(
-            side == 0, jnp.concatenate([kept, arrived], 2), jnp.concatenate([arrived, kept], 2)
-        )
+        pieces += [flip(send, "ctx", 2 * (n + 1)) for n, send in enumerate(sends)]
+        total = sum(pieces[1:], pieces[0])
+
+    with jax.named_scope("return_grads"):
+        rest = [after(arrived, *sends) for arrived in rest]
+        other = [jnp.concatenate([other_dq[n * size : (n + 1) * size], r], 1) for n, r in enumerate(rest)]
+        others[-1] = jnp.concatenate(other, 0)
+        across_other[-1] = jnp.concatenate([flip(o, "head", 1) for o in other], 0)
 
     with jax.named_scope("token_grad"):
         across_all = ordered(across_half, across_rest, core)
@@ -297,15 +316,22 @@
             right = jnp.concatenate([w for _, w in pieces], 1)
             return lax.dot_general(left, right, (((1,), (1,)), ((), ())), preferred_element_type=F32)
 
-        total = None
+        rows_sum = None
         for pair in range(pairs):
             cut = slice(pair * 3 * PAIR, (pair + 1) * 3 * PAIR)
             early = [(wholes[pair][:rows], weight[:, cut]), (across_own[pair], across_weight[:, cut])]
             late = [(others[pair], weight_other[:, cut]), (across_other[pair], across_weight_other[:, cut])]
-            for pieces in ([early, late] if pair == pairs - 1 else [early + late]):
-                term = product(pieces)
-                total = term if total is None else total + term
-        d_tokens = total.astype(BF16)
+            if pair < pairs - 1:
+                early = early + late
+            term = product(early)
+            rows_sum = term if rows_sum is None else rows_sum + term
+        d_tokens = (rows_sum + product(late)).astype(BF16)
+
+    with jax.named_scope("weight_grad"):
+        total = after(total, rows_sum)
+        kept = lax.dynamic_index_in_dim(total, side, 0, keepdims=False)
+        arrived = flip(lax.dynamic_index_in_dim(total, 1 - side, 0, keepdims=False), "ctx", far_mask)
+        d_weight = assemble(side, kept, arrived, d_tokens)
     return (d_tokens, d_weight)
 
 

time: 239 us -> 222 us (0.929)
  local copies, waits for them, and re-layouts: 29.6 us -> 17.6 us
  starting transfers between devices: 43.6 us -> 35.1 us
  waiting for transfers between devices: 70.2 us -> 76.5 us
  other arithmetic: 18.2 us -> 14.6 us
  matrix products: 15.5 us -> 12.2 us
  Pallas kernels: 57.9 us -> 60.8 us
    ppermute x34 -> x31, starting transfers between devices: 43.6 us -> 35.1 us  [flip(): return lax.ppermute(value, axis, pairs)]
    reshape x6 -> x0, local copies, waits for them, and re-layouts: 6.99 us -> none  [on_device(): jnp.stack([t.reshape(shard, 3, PAIR) for t in side_terms], 2)]
    ppermute x34 -> x31, waiting for transfers between devices: 70.2 us -> 76.5 us  [flip(): return lax.ppermute(value, axis, pairs)]
    pallas_call x4 -> x6, Pallas kernels: 57.9 us -> 60.8 us  [the longest x5 58.7 us: attention(): pl.pallas_call(functools.partial(attention_kernel, bool(parts), start, le...]
    dot_general x3, matrix products: 9.03 us -> 6.61 us  [product(): lax.dot_general(left, right, (((1,), (1,)), ((), ())), preferred_element_...]
    unnamed x48 -> x57, local copies, waits for them, and re-layouts: 6.85 us -> 6.64 us
  transfers between devices with their start and end apart: 34 -> 31, of which waited for: 12 -> 11; matrix products, arithmetic and copies ran while one was open for 23% -> 16% of each run, Pallas kernels for 24% -> 24%
where the time goes in v4:
time: 222 us; the launch traced here: 218 us
  waiting for transfers between devices  76.5 us (34%)
  Pallas kernels  60.8 us (27%)
  starting transfers between devices  35.1 us (16%)
  local copies, waits for them, and re-layouts  17.6 us (8%)
  other arithmetic  14.6 us (7%)
  matrix products  12.2 us (5%)
    ppermute x31, waiting for transfers between devices, flip(): return lax.ppermute(value, axis, pairs)  76.5 us
    pallas_call x5, Pallas kernels, attention(): pl.pallas_call(functools.partial(attention_kernel, bool(parts), start, le...  58.7 us
    ppermute x31, starting transfers between devices, flip(): return lax.ppermute(value, axis, pairs)  35.1 us
    unnamed x57, local copies, waits for them, and re-layouts  6.64 us
    dot_general x3, matrix products, product(): lax.dot_general(left, right, (((1,), (1,)), ((), ())), preferred_element_...  6.61 us
    mul x1, other arithmetic, on_device(): jnp.log(jnp.abs(pos[:, None] - pos[None, :]).astype(F32) + 1.0) * LOG2E  6.09 us
  transfers between devices with their start and end apart: 31, of which 11 were waited for; matrix products, arithmetic and copies ran while one was open for 16% of the time, Pallas kernels for 24%

profile of v4, /device:TPU:0, one launch (start us, length us, event | category | flops | bytes accessed | tf_op | source)
XLA Modules:
  0.0 218.4 jit_solution(2584145486955675504)
XLA Ops:
  2.2 4.1 %collective-permute-start = (bf16[64,1536]{1,0:T(8,128)(2,1)S(1)}, bf16[64,1536]{1,0:T(8,128)(2,1)S(1)}, u32[]{:S(2)}, u32[]{:S(2)}) collective-permute-start(bf16[64,1536]{1,0:T(8,128)(2,1)S(1)} %reshape.271), channel_id=1, source_target_pairs={{0,16},{2,18},{4,20},{6,22},{8,24},{10,26},{12,28},{14,30},{16,0},... | collective-permute-start | bytes 589832 | tf_op jit(solution)/shard_map/gather_weight/ppermute | solution.py:20
  8.2 2.9 %collective-permute-start.10 = (s32[768]{0:T(1024)S(1)}, s32[768]{0:T(1024)S(1)}, u32[]{:S(2)}, u32[]{:S(2)}) collective-permute-start(s32[768]{0:T(1024)S(1)} %copy-done.20), channel_id=1, source_target_pairs={{0,16},{2,18},{4,20},{6,22},{8,24},{10,26},{12,28},{14,30},{16,0},... | collective-permute-start | bytes 9224 | tf_op jit(solution)/shard_map/exchange_inputs/ppermute | solution.py:20
  11.4 10.6 %collective-permute-done = bf16[64,1536]{1,0:T(8,128)(2,1)S(1)} collective-permute-done((bf16[64,1536]{1,0:T(8,128)(2,1)S(1)}, bf16[64,1536]{1,0:T(8,128)(2,1)S(1)}, u32[]{:S(2)}, u32[]{:S(2)}) %collective-permute-start) | collective-permute-done | bytes 196640 | tf_op jit(solution)/shard_map/gather_weight/ppermute | solution.py:20
  23.0 3.9 %collective-permute-done.4 = bf16[128,1024]{1,0:T(8,128)(2,1)} collective-permute-done((bf16[128,1024]{1,0:T(8,128)(2,1)S(1)}, bf16[128,1024]{1,0:T(8,128)(2,1)}, u32[]{:S(2)}, u32[]{:S(2)}) %collective-permute-start.4) | collective-permute-done | bytes 262176 | tf_op jit(solution)/shard_map/exchange_inputs/ppermute | solution.py:20
  27.0 12.7 %collective-permute-done.1 = bf16[2,1,64,1536]{3,2,0,1:T(8,128)(2,1)S(1)} collective-permute-done((bf16[2,1,64,1536]{3,2,0,1:T(8,128)(2,1)S(1)}, bf16[2,1,64,1536]{3,2,0,1:T(8,128)(2,1)S(1)}, u32[]{:S(2)}, u32[]{:S(2)}) %collective-permute-start.1) | collective-permute-done | bytes 393248 | tf_op jit(solution)/shard_map/gather_weight/ppermute | solution.py:20
  39.9 2.8 %collective-permute-start.2 = (bf16[2,2,64,1536]{3,2,1,0:T(8,128)(2,1)S(1)}, bf16[2,2,64,1536]{3,2,1,0:T(8,128)(2,1)}, u32[]{:S(2)}, u32[]{:S(2)}) collective-permute-start(bf16[2,2,64,1536]{3,2,1,0:T(8,128)(2,1)S(1)} %maximum_select_fusion.4), channel_id=1, source_target_pairs={{0,4},{2,6},{4,0},{6,2},{8,12},{10,14},{12,8},{14,10},{16,20},{18,... | collective-permute-start | bytes 2359304 | tf_op jit(solution)/shard_map/gather_weight/ppermute | solution.py:20
  45.7 11.3 %collective-permute-done.6 = bf16[128,1024]{1,0:T(8,128)(2,1)S(1)} collective-permute-done((bf16[128,1024]{1,0:T(8,128)(2,1)}, bf16[128,1024]{1,0:T(8,128)(2,1)S(1)}, u32[]{:S(2)}, u32[]{:S(2)}) %collective-permute-start.6) | collective-permute-done | bytes 262176 | tf_op jit(solution)/shard_map/exchange_inputs/ppermute | solution.py:20
  62.3 6.1 %log_multiply_fusion.refs_5_ = f32[1536,1536]{1,0:T(8,128)} fusion(s32[1536]{0:T(1024)S(1)} %constant_dynamic-update-slice_fusion.20), kind=kLoop, calls=%fused_computation | loop fusion | flops 11796480 | bytes 9443328 | tf_op jit(solution)/shard_map/log_distance/mul | solution.py:228
  78.3 3.0 %collective-permute-start.12 = (bf16[768,128]{1,0:T(8,128)(2,1)S(1)}, bf16[768,128]{1,0:T(8,128)(2,1)S(1)}, u32[]{:S(2)}, u32[]{:S(2)}) collective-permute-start(bf16[768,128]{1,0:T(8,128)(2,1)S(1)} %copy-done.15), channel_id=1, source_target_pairs={{0,16},{2,18},{4,20},{6,22},{8,24},{10,26},{12,28},{14,30},{16,0},... | collective-permute-start | bytes 589832 | tf_op jit(solution)/shard_map/exchange_inputs/ppermute | solution.py:20
  81.3 13.9 %attention.5 = (bf16[768,128]{1,0:T(8,128)(2,1)S(1)}, f32[1536,128]{1,0:T(8,128)S(1)}, f32[1536,128]{1,0:T(8,128)S(1)}) custom-call(f32[2]{0:T(128)S(1)} %get-tuple-element.94.refs_0_, bf16[1536,768]{1,0:T(8,128)(2,1)S(1)} %pad_maximum_fusion.refs_1_.refs_2_.refs_3_, bf16[1536,768]{1,0:T(8,128)(2,1)S(1)} %pad_maximum_fusion.refs_1_.refs_2_.refs_3_, ...), custom_call_target="tpu_custom_call" | custom-call | flops 7247757312 | bytes 37748736 | tf_op jit(solution)/shard_map/attention/pallas_call | solution.py:125
  96.3 14.6 %attention.6 = (bf16[1536,384]{1,0:T(8,128)(2,1)S(1)}, bf16[768,256]{1,0:T(8,128)(2,1)S(1)}) custom-call(f32[2]{0:T(128)S(1)} %get-tuple-element.94.refs_0_, bf16[1536,768]{1,0:T(8,128)(2,1)} %copy-done, bf16[1536,768]{1,0:T(8,128)(2,1)} %copy-done, bf16[1536,768]{1,0:T(8,128)(2,1)} %copy-done, bf16[768,128]{1,0:T(8,128)(2,1)S(1)} %get-tuple-element.76.refs_4_, ...), custom_call_target="tpu_custom_call" | custom-call | flops 7247757312 | bytes 37748736 | tf_op jit(solution)/shard_map/attention/pallas_call | solution.py:125
  112.9 2.6 %collective-permute-start.16 = (bf16[768,256]{1,0:T(8,128)(2,1)S(1)}, bf16[768,256]{1,0:T(8,128)(2,1)S(1)}, u32[]{:S(2)}, u32[]{:S(2)}) collective-permute-start(bf16[768,256]{1,0:T(8,128)(2,1)S(1)} %get-tuple-element.36), channel_id=1, source_target_pairs={{0,16},{2,18},{4,20},{6,22},{8,24},{10,26},{12,28},{14,30},{16,0},... | collective-permute-start | bytes 1179656 | tf_op jit(solution)/shard_map/return_grads/ppermute | solution.py:20
  115.5 14.0 %attention.7 = (bf16[768,128]{1,0:T(8,128)(2,1)S(1)}, f32[1536,128]{1,0:T(8,128)S(1)}, f32[1536,128]{1,0:T(8,128)S(1)}) custom-call(f32[2]{0:T(128)S(1)} %get-tuple-element.93.refs_0_, bf16[1536,768]{1,0:T(8,128)(2,1)S(1)} %copy-done.1, bf16[1536,768]{1,0:T(8,128)(2,1)S(1)} %copy-done.1, bf16[1536,768]{1,0:T(8,128)(2,1)S(1)} %copy-done.1, ...), custom_call_target="tpu_custom_call" | custom-call | flops 7247757312 | bytes 37748736 | tf_op jit(solution)/shard_map/attention/pallas_call | solution.py:125
  130.2 5.4 %collective-permute-done.16 = bf16[768,256]{1,0:T(8,128)(2,1)S(1)} collective-permute-done((bf16[768,256]{1,0:T(8,128)(2,1)S(1)}, bf16[768,256]{1,0:T(8,128)(2,1)S(1)}, u32[]{:S(2)}, u32[]{:S(2)}) %collective-permute-start.16) | collective-permute-done | bytes 393248 | tf_op jit(solution)/shard_map/return_grads/ppermute | solution.py:20
  137.1 10.2 %attention.8 = (bf16[512,128]{1,0:T(8,128)(2,1)S(1)}, f32[1536,128]{1,0:T(8,128)S(1)}, f32[1536,128]{1,0:T(8,128)S(1)}) custom-call(f32[2]{0:T(128)S(1)} %get-tuple-element.93.refs_0_, bf16[1536,768]{1,0:T(8,128)(2,1)} %copy-done, bf16[1536,768]{1,0:T(8,128)(2,1)} %copy-done, bf16[1536,768]{1,0:T(8,128)(2,1)} %copy-done, ...), custom_call_target="tpu_custom_call" | custom-call | flops 7247757312 | bytes 37748736 | tf_op jit(solution)/shard_map/attention/pallas_call | solution.py:125
  147.4 3.5 %collective-permute-done.17.refs_10_ = bf16[768,384]{1,0:T(8,128)(2,1)S(1)} collective-permute-done((bf16[768,384]{1,0:T(8,128)(2,1)S(1)}, bf16[768,384]{1,0:T(8,128)(2,1)S(1)}, u32[]{:S(2)}, u32[]{:S(2)}) %collective-permute-start.17) | collective-permute-done | bytes 589856 | tf_op jit(solution)/shard_map/return_grads/ppermute | solution.py:20
  150.9 5.9 %attention.9 = (bf16[1536,384]{1,0:T(8,128)(2,1)S(1)}, bf16[384,256]{1,0:T(8,128)(2,1)S(1)}, bf16[384,256]{1,0:T(8,128)(2,1)S(1)}) custom-call(f32[2]{0:T(128)S(1)} %get-tuple-element.93.refs_0_, bf16[1536,768]{1,0:T(8,128)(2,1)} %copy-done, bf16[1536,768]{1,0:T(8,128)(2,1)} %copy-done, bf16[1536,768]{1,0:T(8,128)(2,1)} %copy-done, ...), custom_call_target="tpu_custom_call" | custom-call | flops 7247757312 | bytes 37748736 | tf_op jit(solution)/shard_map/attention/pallas_call | solution.py:125
  156.8 2.8 %fusion.8 = f32[1024,768]{1,0:T(8,128)S(1)} fusion(bf16[768,1024]{1,0:T(8,128)(2,1)S(1)} %copy-done.11, bf16[768,1024]{1,0:T(8,128)(2,1)S(1)} %copy-done.14, bf16[1536,384]{1,0:T(8,128)(2,1)S(1)} %get-tuple-element.45, bf16[1536,384]{1,0:T(8,128)(2,1)S(1)} %get-tuple-element.35), kind=kOutput, calls=%fused_computation.11 | convolution fusion | flops 2426929152 | bytes 8650752 | tf_op jit(solution)/shard_map/weight_grad/dot_general | solution.py:289
  166.8 2.9 %collective-permute-start.24 = (bf16[384,256]{1,0:T(8,128)(2,1)S(1)}, bf16[384,256]{1,0:T(8,128)(2,1)S(1)}, u32[]{:S(2)}, u32[]{:S(2)}) collective-permute-start(bf16[384,256]{1,0:T(8,128)(2,1)S(1)} %copy-done.4), channel_id=1, source_target_pairs={{0,16},{2,18},{4,20},{6,22},{8,24},{10,26},{12,28},{14,30},{16,0},... | collective-permute-start | bytes 589832 | tf_op jit(solution)/shard_map/return_grads/ppermute | solution.py:20
  172.3 7.1 %collective-permute-done.22 = bf16[384,256]{1,0:T(8,128)(2,1)S(1)} collective-permute-done((bf16[384,256]{1,0:T(8,128)(2,1)S(1)}, bf16[384,256]{1,0:T(8,128)(2,1)S(1)}, u32[]{:S(2)}, u32[]{:S(2)}) %collective-permute-start.22) | collective-permute-done | bytes 196640 | tf_op jit(solution)/shard_map/return_grads/ppermute | solution.py:20
  180.4 3.2 %collective-permute-done.24 = bf16[384,256]{1,0:T(8,128)(2,1)S(1)} collective-permute-done((bf16[384,256]{1,0:T(8,128)(2,1)S(1)}, bf16[384,256]{1,0:T(8,128)(2,1)S(1)}, u32[]{:S(2)}, u32[]{:S(2)}) %collective-permute-start.24) | collective-permute-done | bytes 196640 | tf_op jit(solution)/shard_map/return_grads/ppermute | solution.py:20
  190.9 2.6 %fusion.15 = f32[768,1024]{1,0:T(8,128)S(1)} fusion(f32[768,1024]{1,0:T(8,128)S(1)} %fusion.18, bf16[768,1536]{1,0:T(8,128)(2,1)S(1)} %constant_dynamic-update-slice_fusion.15, bf16[1024,384]{1,0:T(8,128)(2,1)S(1)} %get-tuple-element.63, bf16[1024,384]{1,0:T(8,128)(2,1)S(1)} %get-tuple-element.60, bf16[1024,384]{1,0:T(8,128)(2,1)S(1)} %get-tuple-element.64, ...), kind=kOutput, calls=%fused_computation.20 | convolution fusion | flops 2429288448 | bytes 11796480 | tf_op jit(solution)/shard_map/token_grad/dot_general | solution.py:317
  193.5 7.8 %collective-permute-done.29 = f32[2,64,768]{2,1,0:T(8,128)S(1)} collective-permute-done((f32[2,64,768]{2,1,0:T(8,128)S(1)}, f32[2,64,768]{2,1,0:T(8,128)S(1)}, u32[]{:S(2)}, u32[]{:S(2)}) %collective-permute-start.29) | collective-permute-done | bytes 393248 | tf_op jit(solution)/shard_map/weight_grad/ppermute | solution.py:20
  204.7 8.8 %collective-permute-done.30.arrived_ref = f32[64,768]{1,0:T(8,128)S(1)} collective-permute-done((f32[64,768]{1,0:T(8,128)S(1)}, f32[64,768]{1,0:T(8,128)S(1)}, u32[]{:S(2)}, u32[]{:S(2)}) %collective-permute-start.30) | collective-permute-done | bytes 196640 | tf_op jit(solution)/shard_map/weight_grad/ppermute | solution.py:20
  (149 shorter events, 54.0 us)
Async XLA Ops:
  2.2 19.8 %collective-permute-start = (bf16[64,1536]{1,0:T(8,128)(2,1)S(1)}, bf16[64,1536]{1,0:T(8,128)(2,1)S(1)}, u32[]{:S(2)}, u32[]{:S(2)}) collective-permute-start(bf16[64,1536]{1,0:T(8,128)(2,1)S(1)} %reshape.271), channel_id=1, source_target_pairs={{0,16},{2,18},{4,20},{6,22},{8,24},{10,26},{12,28},{14,30},{16,0},... | collective-permute-start | bytes 589832 | tf_op jit(solution)/shard_map/gather_weight/ppermute | solution.py:20
  8.1 18.8 %collective-permute-start.4 = (bf16[128,1024]{1,0:T(8,128)(2,1)S(1)}, bf16[128,1024]{1,0:T(8,128)(2,1)}, u32[]{:S(2)}, u32[]{:S(2)}) collective-permute-start(bf16[128,1024]{1,0:T(8,128)(2,1)S(1)} %get-tuple-element.73), channel_id=1, source_target_pairs={{0,16},{2,18},{4,20},{6,22},{8,24},{10,26},{12,28},{14,30},{16,0},... | collective-permute-start | bytes 786440 | tf_op jit(solution)/shard_map/exchange_inputs/ppermute | solution.py:20
  8.2 35.2 %collective-permute-start.10 = (s32[768]{0:T(1024)S(1)}, s32[768]{0:T(1024)S(1)}, u32[]{:S(2)}, u32[]{:S(2)}) collective-permute-start(s32[768]{0:T(1024)S(1)} %copy-done.20), channel_id=1, source_target_pairs={{0,16},{2,18},{4,20},{6,22},{8,24},{10,26},{12,28},{14,30},{16,0},... | collective-permute-start | bytes 9224 | tf_op jit(solution)/shard_map/exchange_inputs/ppermute | solution.py:20
  22.0 17.7 %collective-permute-start.1 = (bf16[2,1,64,1536]{3,2,0,1:T(8,128)(2,1)S(1)}, bf16[2,1,64,1536]{3,2,0,1:T(8,128)(2,1)S(1)}, u32[]{:S(2)}, u32[]{:S(2)}) collective-permute-start(bf16[2,1,64,1536]{3,2,0,1:T(8,128)(2,1)S(1)} %fusion.57), channel_id=1, source_target_pairs={{0,8},{2,10},{4,12},{6,14},{8,0},{10,2},{12,4},{14,6},{16,24},{18,... | collective-permute-start | bytes 1179656 | tf_op jit(solution)/shard_map/gather_weight/ppermute | solution.py:20
  27.0 16.4 %collective-permute-start.5 = (bf16[128,1024]{1,0:T(8,128)(2,1)S(1)}, bf16[128,1024]{1,0:T(8,128)(2,1)}, u32[]{:S(2)}, u32[]{:S(2)}) collective-permute-start(bf16[128,1024]{1,0:T(8,128)(2,1)S(1)} %get-tuple-element.27), channel_id=1, source_target_pairs={{0,16},{2,18},{4,20},{6,22},{8,24},{10,26},{12,28},{14,30},{16,0},... | collective-permute-start | bytes 786440 | tf_op jit(solution)/shard_map/exchange_inputs/ppermute | solution.py:20
  39.9 20.6 %collective-permute-start.2 = (bf16[2,2,64,1536]{3,2,1,0:T(8,128)(2,1)S(1)}, bf16[2,2,64,1536]{3,2,1,0:T(8,128)(2,1)}, u32[]{:S(2)}, u32[]{:S(2)}) collective-permute-start(bf16[2,2,64,1536]{3,2,1,0:T(8,128)(2,1)S(1)} %maximum_select_fusion.4), channel_id=1, source_target_pairs={{0,4},{2,6},{4,0},{6,2},{8,12},{10,14},{12,8},{14,10},{16,20},{18,... | collective-permute-start | bytes 2359304 | tf_op jit(solution)/shard_map/gather_weight/ppermute | solution.py:20
  43.5 24.9 %collective-permute-start.7 = (bf16[128,1024]{1,0:T(8,128)(2,1)}, bf16[128,1024]{1,0:T(8,128)(2,1)S(1)}, u32[]{:S(2)}, u32[]{:S(2)}) collective-permute-start(bf16[128,1024]{1,0:T(8,128)(2,1)} %collective-permute-done.4), channel_id=1, source_target_pairs={{0,1},{1,0},{2,3},{3,2},{4,5},{5,4},{6,7},{7,6},{8,9},{9,8},{10,11... | collective-permute-start | bytes 786440 | tf_op jit(solution)/shard_map/exchange_inputs/ppermute | solution.py:20
  45.1 23.4 %collective-permute-start.8 = (bf16[128,1024]{1,0:T(8,128)(2,1)}, bf16[128,1024]{1,0:T(8,128)(2,1)S(1)}, u32[]{:S(2)}, u32[]{:S(2)}) collective-permute-start(bf16[128,1024]{1,0:T(8,128)(2,1)} %collective-permute-done.5), channel_id=1, source_target_pairs={{0,1},{1,0},{2,3},{3,2},{4,5},{5,4},{6,7},{7,6},{8,9},{9,8},{10,11... | collective-permute-start | bytes 786440 | tf_op jit(solution)/shard_map/exchange_inputs/ppermute | solution.py:20
  76.3 20.0 %collective-permute-start.13 = (bf16[256,1536]{1,0:T(8,128)(2,1)S(1)}, bf16[256,1536]{1,0:T(8,128)(2,1)S(1)}, u32[]{:S(2)}, u32[]{:S(2)}) collective-permute-start(bf16[256,1536]{1,0:T(8,128)(2,1)S(1)} %get-tuple-element.69), channel_id=1, source_target_pairs={{0,1},{1,0},{2,3},{3,2},{4,5},{5,4},{6,7},{7,6},{8,9},{9,8},{10,11... | collective-permute-start | bytes 2359304 | tf_op jit(solution)/shard_map/gather_other_weight/ppermute | solution.py:20
  78.3 18.0 %collective-permute-start.12 = (bf16[768,128]{1,0:T(8,128)(2,1)S(1)}, bf16[768,128]{1,0:T(8,128)(2,1)S(1)}, u32[]{:S(2)}, u32[]{:S(2)}) collective-permute-start(bf16[768,128]{1,0:T(8,128)(2,1)S(1)} %copy-done.15), channel_id=1, source_target_pairs={{0,16},{2,18},{4,20},{6,22},{8,24},{10,26},{12,28},{14,30},{16,0},... | collective-permute-start | bytes 589832 | tf_op jit(solution)/shard_map/exchange_inputs/ppermute | solution.py:20
  95.3 20.3 %collective-permute-start.15 = (bf16[768,128]{1,0:T(8,128)(2,1)S(1)}, bf16[768,128]{1,0:T(8,128)(2,1)S(1)}, u32[]{:S(2)}, u32[]{:S(2)}) collective-permute-start(bf16[768,128]{1,0:T(8,128)(2,1)S(1)} %get-tuple-element.32.refs_8_), channel_id=1, source_target_pairs={{0,16},{2,18},{4,20},{6,22},{8,24},{10,26},{12,28},{14,30},{16,0},... | collective-permute-start | bytes 589832 | tf_op jit(solution)/shard_map/return_grads/ppermute | solution.py:20
  96.1 41.0 %collective-permute-start.18 = (bf16[256,1536]{1,0:T(8,128)(2,1)S(1)}, bf16[256,1536]{1,0:T(8,128)(2,1)S(1)}, u32[]{:S(2)}, u32[]{:S(2)}) collective-permute-start(bf16[256,1536]{1,0:T(8,128)(2,1)S(1)} %get-tuple-element.39), channel_id=1, source_target_pairs={{0,1},{1,0},{2,3},{3,2},{4,5},{5,4},{6,7},{7,6},{8,9},{9,8},{10,11... | collective-permute-start | bytes 2359304 | tf_op jit(solution)/shard_map/gather_other_weight/ppermute | solution.py:20
  111.1 18.9 %collective-permute-start.14 = (bf16[768,384]{1,0:T(8,128)(2,1)S(1)}, bf16[768,384]{1,0:T(8,128)(2,1)S(1)}, u32[]{:S(2)}, u32[]{:S(2)}) collective-permute-start(bf16[768,384]{1,0:T(8,128)(2,1)S(1)} %get-tuple-element.75), channel_id=1, source_target_pairs={{0,1},{1,0},{2,3},{3,2},{4,5},{5,4},{6,7},{7,6},{8,9},{9,8},{10,11... | collective-permute-start | bytes 1769480 | tf_op jit(solution)/shard_map/return_grads/ppermute | solution.py:20
  112.9 22.6 %collective-permute-start.16 = (bf16[768,256]{1,0:T(8,128)(2,1)S(1)}, bf16[768,256]{1,0:T(8,128)(2,1)S(1)}, u32[]{:S(2)}, u32[]{:S(2)}) collective-permute-start(bf16[768,256]{1,0:T(8,128)(2,1)S(1)} %get-tuple-element.36), channel_id=1, source_target_pairs={{0,16},{2,18},{4,20},{6,22},{8,24},{10,26},{12,28},{14,30},{16,0},... | collective-permute-start | bytes 1179656 | tf_op jit(solution)/shard_map/return_grads/ppermute | solution.py:20
  129.6 17.8 %collective-permute-start.19 = (bf16[768,128]{1,0:T(8,128)(2,1)S(1)}, bf16[768,128]{1,0:T(8,128)(2,1)S(1)}, u32[]{:S(2)}, u32[]{:S(2)}) collective-permute-start(bf16[768,128]{1,0:T(8,128)(2,1)S(1)} %get-tuple-element.37.refs_8_), channel_id=1, source_target_pairs={{0,16},{2,18},{4,20},{6,22},{8,24},{10,26},{12,28},{14,30},{16,0},... | collective-permute-start | bytes 589832 | tf_op jit(solution)/shard_map/return_grads/ppermute | solution.py:20
  135.6 15.2 %collective-permute-start.17 = (bf16[768,384]{1,0:T(8,128)(2,1)S(1)}, bf16[768,384]{1,0:T(8,128)(2,1)S(1)}, u32[]{:S(2)}, u32[]{:S(2)}) collective-permute-start(bf16[768,384]{1,0:T(8,128)(2,1)S(1)} %get-tuple-element.38.refs_8_), channel_id=1, source_target_pairs={{0,1},{1,0},{2,3},{3,2},{4,5},{5,4},{6,7},{7,6},{8,9},{9,8},{10,11... | collective-permute-start | bytes 1769480 | tf_op jit(solution)/shard_map/return_grads/ppermute | solution.py:20
  162.4 22.0 %collective-permute-start.20 = (bf16[512,1536]{1,0:T(8,128)(2,1)}, bf16[512,1536]{1,0:T(8,128)(2,1)}, u32[]{:S(2)}, u32[]{:S(2)}) collective-permute-start(bf16[512,1536]{1,0:T(8,128)(2,1)} %pad_maximum_fusion.1), channel_id=1, source_target_pairs={{0,2},{2,0},{4,6},{6,4},{8,10},{10,8},{12,14},{14,12},{16,18},{18,... | collective-permute-start | bytes 4718600 | tf_op jit(solution)/shard_map/gather_other_weight/ppermute | solution.py:20
  165.3 22.6 %collective-permute-start.21 = (bf16[768,384]{1,0:T(8,128)(2,1)S(1)}, bf16[768,384]{1,0:T(8,128)(2,1)S(1)}, u32[]{:S(2)}, u32[]{:S(2)}) collective-permute-start(bf16[768,384]{1,0:T(8,128)(2,1)S(1)} %slice.94), channel_id=1, source_target_pairs={{0,1},{1,0},{2,3},{3,2},{4,5},{5,4},{6,7},{7,6},{8,9},{9,8},{10,11... | collective-permute-start | bytes 1769480 | tf_op jit(solution)/shard_map/return_grads/ppermute | solution.py:20
  166.8 16.9 %collective-permute-start.24 = (bf16[384,256]{1,0:T(8,128)(2,1)S(1)}, bf16[384,256]{1,0:T(8,128)(2,1)S(1)}, u32[]{:S(2)}, u32[]{:S(2)}) collective-permute-start(bf16[384,256]{1,0:T(8,128)(2,1)S(1)} %copy-done.4), channel_id=1, source_target_pairs={{0,16},{2,18},{4,20},{6,22},{8,24},{10,26},{12,28},{14,30},{16,0},... | collective-permute-start | bytes 589832 | tf_op jit(solution)/shard_map/return_grads/ppermute | solution.py:20
  171.6 21.9 %collective-permute-start.27 = (f32[2,64,768]{2,1,0:T(8,128)S(1)}, f32[2,64,768]{2,1,0:T(8,128)S(1)}, u32[]{:S(2)}, u32[]{:S(2)}) collective-permute-start(f32[2,64,768]{2,1,0:T(8,128)S(1)} %get-tuple-element.68), channel_id=1, source_target_pairs={{0,4},{2,6},{4,0},{6,2},{8,12},{10,14},{12,8},{14,10},{16,20},{18,... | collective-permute-start | bytes 1179656 | tf_op jit(solution)/shard_map/weight_grad/ppermute | solution.py:20
  179.4 14.1 %collective-permute-start.28 = (f32[2,64,768]{2,1,0:T(8,128)S(1)}, f32[2,64,768]{2,1,0:T(8,128)S(1)}, u32[]{:S(2)}, u32[]{:S(2)}) collective-permute-start(f32[2,64,768]{2,1,0:T(8,128)S(1)} %get-tuple-element.67), channel_id=1, source_target_pairs={{0,8},{2,10},{4,12},{6,14},{8,0},{10,2},{12,4},{14,6},{16,24},{18,... | collective-permute-start | bytes 1179656 | tf_op jit(solution)/shard_map/weight_grad/ppermute | solution.py:20
  183.6 17.6 %collective-permute-start.29 = (f32[2,64,768]{2,1,0:T(8,128)S(1)}, f32[2,64,768]{2,1,0:T(8,128)S(1)}, u32[]{:S(2)}, u32[]{:S(2)}) collective-permute-start(f32[2,64,768]{2,1,0:T(8,128)S(1)} %get-tuple-element.66), channel_id=1, source_target_pairs={{0,12},{2,14},{4,8},{6,10},{8,4},{10,6},{12,0},{14,2},{16,28},{18,... | collective-permute-start | bytes 1179656 | tf_op jit(solution)/shard_map/weight_grad/ppermute | solution.py:20
  184.4 17.7 %collective-permute-start.25 = (bf16[384,384]{1,0:T(8,128)(2,1)S(1)}, bf16[384,384]{1,0:T(8,128)(2,1)S(1)}, u32[]{:S(2)}, u32[]{:S(2)}) collective-permute-start(bf16[384,384]{1,0:T(8,128)(2,1)S(1)} %pad_maximum_fusion.3), channel_id=1, source_target_pairs={{0,1},{1,0},{2,3},{3,2},{4,5},{5,4},{6,7},{7,6},{8,9},{9,8},{10,11... | collective-permute-start | bytes 884744 | tf_op jit(solution)/shard_map/return_grads/ppermute | solution.py:20
  187.9 14.2 %collective-permute-start.26 = (bf16[384,384]{1,0:T(8,128)(2,1)S(1)}, bf16[384,384]{1,0:T(8,128)(2,1)S(1)}, u32[]{:S(2)}, u32[]{:S(2)}) collective-permute-start(bf16[384,384]{1,0:T(8,128)(2,1)S(1)} %pad_maximum_fusion.4), channel_id=1, source_target_pairs={{0,1},{1,0},{2,3},{3,2},{4,5},{5,4},{6,7},{7,6},{8,9},{9,8},{10,11... | collective-permute-start | bytes 884744 | tf_op jit(solution)/shard_map/return_grads/ppermute | solution.py:20
  (29 other events, 241.4 us)
